TPU v7x, 128 devices: a whole 4x4x4 slice. The times are simulated.
128 devices in a mesh: brow: 8 (over x, core), bcol: 16 (over z, y).
Axes of the slice: x: 4, y: 4, z: 4, core: 2. Of those that a mesh axis runs over, the one named last changes fastest.
Arguments:
- forcing: bfloat16 [62, 8192, 2048], P(None, 'brow', 'bcol'), may hold values from -6 to 6
- bottom_level: int32 [8192, 2048], P('brow', 'bcol'), may hold values from 0 to 62
- thickness: float32 [62], replicated, may hold values from 0.25 to 4
- eta_prev: float32 [8, 224, 64, 128], P('brow', 'bcol'), may hold values from -6 to 6
- tropic_map: int32 [128, 16], replicated, may hold values from -1 to 223, as said below
Outputs:
- eta_next: float32 [8, 224, 64, 128], P('brow', 'bcol')
Inputs may be any that keep to these rules, and one draw needn't show every extreme that they name: `tropic_map`: each block's owner lies in the band of the block (block rows b * 16 to b * 16 + 15 belong to brow index b); a wet block's value is the owner's bcol index times 14 plus its slot there. Every device owns exactly 14 wet blocks, one in each slot. No clinic device gives more than 2 of its blocks to one owner, and in every band some clinic device gives exactly 2 to some owner.
All inputs are finite; a program needn't handle non-finite values.
Results may differ from a plain program's by a relative error of at most 0.0003.
Values sent between devices are 32-bit elements; how exact they have to be, the bound alone decides.
A program may use at most 128 MiB of HBM per device.

v0:
```python
import math

import jax
import jax.numpy as jnp
from jax import lax
from jax.sharding import PartitionSpec as P

ITERS = 4
PEER_MOST = 2


surface_term = 0.25
neighbour_offsets = (
    (-1, 0, 1.0),
    (1, 0, 1.0),
    (0, -1, 1.0),
    (0, 1, 1.0),
    (-1, -1, 0.5),
    (-1, 1, 0.5),
    (1, -1, 0.5),
    (1, 1, 0.5),
)


def padded_2(array, sides, width):
    for axis, dim in sides:
        size, length = (lax.axis_size(axis), array.shape[dim])
        up = [(i, (i + 1) % size) for i in range(size - 1)]
        down = [(j, i) for i, j in up]
        last = lax.slice_in_dim(array, length - width, length, axis=dim)
        leading = lax.slice_in_dim(array, 0, width, axis=dim)
        before = lax.ppermute(last, axis, up)
        after = lax.ppermute(leading, axis, down)
        array = jnp.concatenate([before, array, after], axis=dim)
    return array


def shifted(padded, row_shift, col_shift, height, width):
    return padded[
        ..., 1 + row_shift : 1 + row_shift + height, 1 + col_shift : 1 + col_shift + width
    ]


def couplings(depth, padded_depth):
    height, width = (depth.shape[-2], depth.shape[-1])
    terms = []
    diagonal = surface_term + depth
    for row_shift, col_shift, weight in neighbour_offsets:
        term = weight * (depth + shifted(padded_depth, row_shift, col_shift, height, width)) * 0.5
        terms.append(term)
        diagonal = diagonal + term
    return (terms, diagonal)


def jacobi_sweep(padded_eta, rhs, terms, diagonal):
    height, width = (rhs.shape[-2], rhs.shape[-1])
    total = rhs
    for (row_shift, col_shift, weight), term in zip(neighbour_offsets, terms):
        total = total + term * shifted(padded_eta, row_shift, col_shift, height, width)
    return total / diagonal


def publish(field):
    pieces = (
        field[:, -1, :],
        field[:, 0, :],
        field[:, :, -1],
        field[:, :, 0],
        field[:, -1, -1:],
        field[:, -1, :1],
        field[:, 0, -1:],
        field[:, 0, :1],
    )
    return jnp.concatenate(pieces, axis=1)


def assemble(center, picked):
    block_rows = center.shape[1]
    block_cols = center.shape[2]
    corner_start = 2 * block_cols + 2 * block_rows
    lower = picked[:, 0, 0:block_cols]
    upper = picked[:, 1, block_cols : 2 * block_cols]
    left_side = picked[:, 2, 2 * block_cols : 2 * block_cols + block_rows]
    right_side = picked[:, 3, 2 * block_cols + block_rows : corner_start]
    lower_left = picked[:, 4, corner_start : corner_start + 1]
    lower_right = picked[:, 5, corner_start + 1 : corner_start + 2]
    upper_left = picked[:, 6, corner_start + 2 : corner_start + 3]
    upper_right = picked[:, 7, corner_start + 3 : corner_start + 4]
    bottom_row = jnp.concatenate(
        [lower_left[:, None, :], lower[:, None, :], lower_right[:, None, :]], axis=2
    )
    middle = jnp.concatenate([left_side[:, :, None], center, right_side[:, :, None]], axis=2)
    top_row = jnp.concatenate(
        [upper_left[:, None, :], upper[:, None, :], upper_right[:, None, :]], axis=2
    )
    return jnp.concatenate([bottom_row, middle, top_row], axis=1)


def body(forcing, bottom_level, thickness, eta_prev, tropic_map):
    level_count = forcing.shape[0]
    region_rows = forcing.shape[1]
    slot_count = eta_prev.shape[1]
    block_rows = eta_prev.shape[2]
    block_cols = eta_prev.shape[3]
    block_cells = block_rows * block_cols
    band_rows = region_rows // block_rows
    column_count = tropic_map.shape[1]
    capacity = column_count * PEER_MOST
    my_column = lax.axis_index("bcol")
    band_map = lax.dynamic_slice_in_dim(
        tropic_map, lax.axis_index("brow") * band_rows, band_rows, 0
    )
    row_ids = jnp.arange(band_rows, dtype=jnp.int32)[:, None] * jnp.ones(
        (1, column_count), jnp.int32
    )
    column_ids = (
        jnp.ones((band_rows, 1), jnp.int32) * jnp.arange(column_count, dtype=jnp.int32)[None, :]
    )
    wet_band = band_map >= 0
    owner = jnp.where(wet_band, band_map // slot_count, -1)
    slot_of = jnp.where(wet_band, band_map % slot_count, -1)
    earlier = jnp.arange(band_rows)[:, None] < jnp.arange(band_rows)[None, :]
    same_owner = (
        (owner[:, None, :] == owner[None, :, :]) & wet_band[:, None, :] & earlier[:, :, None]
    )
    rank = jnp.sum(same_owner.astype(jnp.int32), axis=0)
    own_pick = column_ids == my_column
    own_owner = jnp.sum(jnp.where(own_pick, owner, 0), axis=1)
    own_rank = jnp.sum(jnp.where(own_pick, rank, 0), axis=1)
    own_wet = jnp.any(own_pick & wet_band, axis=1)
    send_slot = own_owner * PEER_MOST + own_rank
    buffer_ids = jnp.arange(capacity, dtype=jnp.int32)
    sender_table = ((buffer_ids[:, None] == send_slot[None, :]) & own_wet[None, :]).astype(
        jnp.float32
    )
    mine = wet_band & (owner == my_column)
    arrival = (column_ids * PEER_MOST + rank).reshape(-1)
    slot_ids = jnp.arange(slot_count, dtype=jnp.int32)
    slot_match = mine[None] & (slot_of[None] == slot_ids[:, None, None])
    receiver_table = jnp.dot(
        slot_match.reshape(slot_count, -1).astype(jnp.float32),
        (arrival[:, None] == buffer_ids[None, :]).astype(jnp.float32),
        precision=lax.Precision.HIGHEST,
        preferred_element_type=jnp.float32,
    )
    level_ids = jnp.arange(level_count, dtype=jnp.int32)[:, None, None]
    wet_level = level_ids < bottom_level[None, :, :]
    layer_thickness = thickness[:, None, None]
    depth = jnp.sum(jnp.where(wet_level, layer_thickness, 0.0), axis=0) / level_count
    source = jnp.sum(jnp.where(wet_level, layer_thickness * forcing, 0.0), axis=0) / math.sqrt(
        level_count
    )
    cell_mask = jnp.repeat(own_wet.astype(jnp.float32), block_rows)[:, None]
    depth = depth * cell_mask
    source = source * cell_mask
    my_row = jnp.sum(jnp.where(slot_match, row_ids[None], 0), axis=(1, 2))
    my_col = jnp.sum(jnp.where(slot_match, column_ids[None], 0), axis=(1, 2))
    zero_entry = 2 * column_count + column_count * slot_count
    entries = []
    for row_shift, col_shift, weight in neighbour_offsets:
        target_row = my_row + row_shift
        target_col = (my_col + col_shift) % column_count
        hit = (row_ids[None] == target_row[:, None, None]) & (
            column_ids[None] == target_col[:, None, None]
        )
        found = jnp.sum(jnp.where(hit, band_map[None], 0), axis=(1, 2))
        inside = jnp.where(found >= 0, column_count + found, zero_entry)
        upper_entry = column_count + column_count * slot_count + target_col
        entries.append(
            jnp.where(
                target_row < 0, target_col, jnp.where(target_row >= band_rows, upper_entry, inside)
            )
        )
    neighbour_index = jnp.stack(entries, axis=1).reshape(-1)
    own_slots = column_count * slot_count
    first_index = jnp.where(band_map[0] >= 0, band_map[0], own_slots)
    last_index = jnp.where(band_map[band_rows - 1] >= 0, band_map[band_rows - 1], own_slots)

    def tropic_halo(field):
        published = publish(field)
        rim_width = published.shape[1]
        band_table = lax.all_gather(published, "bcol", axis=0, tiled=True)
        zero_row = jnp.zeros((1, rim_width), jnp.float32)
        with_zero = jnp.concatenate([band_table, zero_row], axis=0)
        edges = jnp.stack(
            [jnp.take(with_zero, first_index, axis=0), jnp.take(with_zero, last_index, axis=0)],
            axis=0,
        )
        beside_all = padded_2(edges, (("brow", 0),), 1)
        table = jnp.concatenate([beside_all[0], band_table, beside_all[3], zero_row], axis=0)
        picked = jnp.take(table, neighbour_index, axis=0).reshape(slot_count, 8, rim_width)
        return assemble(field, picked)

    both_fields = jnp.concatenate(
        [depth.reshape(band_rows, block_cells), source.reshape(band_rows, block_cells)], axis=1
    )
    outgoing = jnp.dot(
        sender_table,
        both_fields,
        precision=lax.Precision.HIGHEST,
        preferred_element_type=jnp.float32,
    )
    incoming = lax.all_to_all(outgoing, "bcol", split_axis=0, concat_axis=0, tiled=True)
    moved = jnp.dot(
        receiver_table,
        incoming,
        precision=lax.Precision.HIGHEST,
        preferred_element_type=jnp.float32,
    )
    tropic_depth = moved[:, :block_cells].reshape(slot_count, block_rows, block_cols)
    tropic_source = moved[:, block_cells:].reshape(slot_count, block_rows, block_cols)
    terms, diagonal = couplings(tropic_depth, tropic_halo(tropic_depth))
    eta = eta_prev.reshape(slot_count, block_rows, block_cols)
    rhs = (surface_term + tropic_depth) * eta + tropic_source
    for iteration in range(ITERS):
        eta = jacobi_sweep(tropic_halo(eta), rhs, terms, diagonal)
    return eta.reshape(1, slot_count, block_rows, block_cols)


def solution(mesh):
    in_specs = (P(None, "brow", "bcol"), P("brow", "bcol"), P(), P("brow", "bcol", None, None), P())
    out_specs = P("brow", "bcol", None, None)
    return jax.shard_map(body, mesh=mesh, in_specs=in_specs, out_specs=out_specs, check_vma=False)
```

profile of v0, /device:TPU:1, one launch (start us, length us, event | category | flops | bytes accessed | tf_op | source)
XLA Modules:
  0.0 292.2 jit_solution(10183438463114247265)
XLA Ops:
  1.0 11.1 %select_reduce_fusion.1 = (f32[1024,128]{1,0:T(8,128)S(1)}, f32[1024,128]{1,0:T(8,128)S(1)}) fusion(f32[62]{0:T(128)} %param.11, s32[1024,128]{1,0:T(8,128)} %param.10, bf16[62,1024,128]{2,1,0:T(8,128)(2,1)} %param.9), kind=kLoop, calls=%fused_computation.16 | loop fusion | flops 56623104 | bytes 17826040 | tf_op jit(solution)/shard_map/reduce_sum | solution.py:149
  13.8 2.3 all_to_all.8
  16.0 8.8 %all-to-all-start = ((f32[16,2,16384]{2,1,0:T(2,128)}), f32[16,2,16384]{2,1,0:T(2,128)}, u32[]{:S(2)}, u32[]{:S(2)}) async-start(f32[16,2,16384]{2,1,0:T(2,128)} %all_to_all.8), calls=%async_computation | async-start | bytes 4194304 | tf_op jit(solution)/shard_map/all_to_all | solution.py:203
  25.4 2.3 select_reduce_fusion.2
  29.4 37.1 %all-gather.1 = f32[16,14,388]{2,1,0:T(8,128)S(1)} all-gather(f32[1,14,388]{2,1,0:T(8,128)S(1)} %bitcast.279), channel_id=1, replica_groups=mesh['brow'=8,'bcol'=16] {'bcol'}, dimensions={0}, use_global_device_ids=true | all-gather | bytes 369376 | tf_op jit(solution)/shard_map/all_gather | solution.py:182
  66.6 1.2 gather_fusion.4
  69.8 3.7 %all_to_all.10 = f32[32,16384]{1,0:T(8,128)} reshape(f32[16,2,16384]{2,1,0:T(2,128)} %all-to-all-done) | data formatting | bytes 4194304 | tf_op jit(solution)/shard_map/all_to_all | solution.py:203
  73.4 2.7 fusion.114
  78.2 17.2 %all-gather = f32[16,14,388]{2,1,0:T(8,128)S(1)} all-gather(f32[1,14,388]{2,1,0:T(8,128)S(1)} %bitcast.280), channel_id=1, replica_groups=mesh['brow'=8,'bcol'=16] {'bcol'}, dimensions={0}, use_global_device_ids=true | all-gather | bytes 369376 | tf_op jit(solution)/shard_map/all_gather | solution.py:182
  97.4 12.6 %collective-permute-start.1 = (f32[1,16,388]{2,1,0:T(8,128)S(1)}, f32[1,16,388]{2,1,0:T(8,128)S(1)}, u32[]{:S(2)}, u32[]{:S(2)}) collective-permute-start(f32[1,16,388]{2,1,0:T(8,128)S(1)} %get-tuple-element.140), channel_id=1, source_target_pairs={{16,0},{32,16},{48,32},{64,48},{80,64},{96,80},{112,96},{17,1},{33... | collective-permute-start | bytes 74504 | tf_op jit(solution)/shard_map/ppermute | solution.py:33
  110.0 1.9 collective-permute-start.3
  112.0 3.6 %collective-permute-start = (f32[1,16,388]{2,1,0:T(8,128)S(1)}, f32[1,16,388]{2,1,0:T(8,128)S(1)}, u32[]{:S(2)}, u32[]{:S(2)}) collective-permute-start(f32[1,16,388]{2,1,0:T(8,128)S(1)} %get-tuple-element.138), channel_id=1, source_target_pairs={{0,16},{16,32},{32,48},{48,64},{64,80},{80,96},{96,112},{1,17},{17... | collective-permute-start | bytes 74504 | tf_op jit(solution)/shard_map/ppermute | solution.py:32
  115.6 2.1 collective-permute-start.2
  121.7 1.1 copy.503
  126.7 2.8 fusion.39
  129.6 1.1 fusion.100
  130.7 1.3 copy.536
  132.0 1.3 copy.535
  133.4 19.2 %all-gather.2 = f32[16,14,388]{2,1,0:T(8,128)} all-gather(f32[1,14,388]{2,1,0:T(8,128)S(1)} %bitcast.281), channel_id=1, replica_groups=mesh['brow'=8,'bcol'=16] {'bcol'}, dimensions={0}, use_global_device_ids=true | all-gather | bytes 369376 | tf_op jit(solution)/shard_map/all_gather | solution.py:182
  152.6 1.9 reshape.711
  154.4 1.8 concatenate.200
  156.3 1.6 gather_fusion.7
  157.9 1.6 gather_fusion.6
  159.7 7.9 %collective-permute-start.5 = (f32[1,16,388]{2,1,0:T(8,128)S(1)}, f32[1,16,388]{2,1,0:T(8,128)S(1)}, u32[]{:S(2)}, u32[]{:S(2)}) collective-permute-start(f32[1,16,388]{2,1,0:T(8,128)S(1)} %select_bitcast_fusion.9), channel_id=1, source_target_pairs={{16,0},{32,16},{48,32},{64,48},{80,64},{96,80},{112,96},{17,1},{33... | collective-permute-start | bytes 74504 | tf_op jit(solution)/shard_map/ppermute | solution.py:33
  167.5 3.5 %collective-permute-start.4 = (f32[1,16,388]{2,1,0:T(8,128)S(1)}, f32[1,16,388]{2,1,0:T(8,128)S(1)}, u32[]{:S(2)}, u32[]{:S(2)}) collective-permute-start(f32[1,16,388]{2,1,0:T(8,128)S(1)} %select_bitcast_fusion.10), channel_id=1, source_target_pairs={{0,16},{16,32},{32,48},{48,64},{64,80},{80,96},{96,112},{1,17},{17... | collective-permute-start | bytes 74504 | tf_op jit(solution)/shard_map/ppermute | solution.py:32
  171.1 1.0 collective-permute-done.4
  172.1 1.9 maximum_maximum_fusion.12
  174.0 1.9 gather_fusion.8
  176.3 1.1 copy.544
  177.3 1.1 copy.545
  178.4 2.9 maximum_maximum_fusion.4
  181.4 2.0 fusion.28
  183.5 1.1 fusion.99
  184.6 1.3 copy.552
  185.9 1.3 copy.551
  187.3 19.7 %all-gather.3 = f32[16,14,388]{2,1,0:T(8,128)} all-gather(f32[1,14,388]{2,1,0:T(8,128)S(1)} %bitcast.282), channel_id=1, replica_groups=mesh['brow'=8,'bcol'=16] {'bcol'}, dimensions={0}, use_global_device_ids=true | all-gather | bytes 369376 | tf_op jit(solution)/shard_map/all_gather | solution.py:182
  206.9 1.9 reshape.713
  208.8 1.8 concatenate.210
  210.6 1.6 gather_fusion.10
  212.2 1.6 gather_fusion.9
  214.0 5.4 %collective-permute-start.7 = (f32[1,16,388]{2,1,0:T(8,128)S(1)}, f32[1,16,388]{2,1,0:T(8,128)S(1)}, u32[]{:S(2)}, u32[]{:S(2)}) collective-permute-start(f32[1,16,388]{2,1,0:T(8,128)S(1)} %select_bitcast_fusion.7), channel_id=1, source_target_pairs={{16,0},{32,16},{48,32},{64,48},{80,64},{96,80},{112,96},{17,1},{33... | collective-permute-start | bytes 74504 | tf_op jit(solution)/shard_map/ppermute | solution.py:33
  219.4 5.5 %collective-permute-start.6 = (f32[1,16,388]{2,1,0:T(8,128)S(1)}, f32[1,16,388]{2,1,0:T(8,128)S(1)}, u32[]{:S(2)}, u32[]{:S(2)}) collective-permute-start(f32[1,16,388]{2,1,0:T(8,128)S(1)} %select_bitcast_fusion.8), channel_id=1, source_target_pairs={{0,16},{16,32},{32,48},{48,64},{64,80},{80,96},{96,112},{1,17},{17... | collective-permute-start | bytes 74504 | tf_op jit(solution)/shard_map/ppermute | solution.py:32
  225.9 1.9 maximum_maximum_fusion.13
  227.8 1.9 gather_fusion.11
  230.1 1.1 copy.560
  231.2 1.1 copy.561
  232.3 2.9 maximum_maximum_fusion.6
  235.2 2.0 fusion.17
  237.3 1.1 fusion.98
  238.4 1.3 copy.568
  239.7 1.3 copy.567
  241.1 19.7 %all-gather.4 = f32[16,14,388]{2,1,0:T(8,128)} all-gather(f32[1,14,388]{2,1,0:T(8,128)S(1)} %bitcast.283), channel_id=1, replica_groups=mesh['brow'=8,'bcol'=16] {'bcol'}, dimensions={0}, use_global_device_ids=true | all-gather | bytes 369376 | tf_op jit(solution)/shard_map/all_gather | solution.py:182
  260.8 1.9 reshape.715
  262.7 1.8 concatenate.220
  264.5 1.6 gather_fusion.13
  266.1 1.6 gather_fusion.12
  267.9 4.1 %collective-permute-start.9 = (f32[1,16,388]{2,1,0:T(8,128)S(1)}, f32[1,16,388]{2,1,0:T(8,128)S(1)}, u32[]{:S(2)}, u32[]{:S(2)}) collective-permute-start(f32[1,16,388]{2,1,0:T(8,128)S(1)} %select_bitcast_fusion.5), channel_id=1, source_target_pairs={{16,0},{32,16},{48,32},{64,48},{80,64},{96,80},{112,96},{17,1},{33... | collective-permute-start | bytes 74504 | tf_op jit(solution)/shard_map/ppermute | solution.py:33
  272.0 7.0 %collective-permute-start.8 = (f32[1,16,388]{2,1,0:T(8,128)S(1)}, f32[1,16,388]{2,1,0:T(8,128)S(1)}, u32[]{:S(2)}, u32[]{:S(2)}) collective-permute-start(f32[1,16,388]{2,1,0:T(8,128)S(1)} %select_bitcast_fusion.6), channel_id=1, source_target_pairs={{0,16},{16,32},{32,48},{48,64},{64,80},{80,96},{96,112},{1,17},{17... | collective-permute-start | bytes 74504 | tf_op jit(solution)/shard_map/ppermute | solution.py:32
  280.0 1.9 maximum_maximum_fusion.14
  281.9 1.9 gather_fusion.14
  284.1 1.1 copy.576
  285.2 1.1 copy.577
  286.3 2.9 maximum_maximum_fusion.8
  289.2 2.0 fusion.6
  (231 shorter events, 23.3 us)
Async XLA Ops:
  0.0 0.7 copy-start
  16.0 12.2 %copy-start.30 = (f32[1,14,64,128]{3,2,1,0:T(8,128)S(1)}, f32[1,14,64,128]{3,2,1,0:T(8,128)}, u32[]{:S(2)}) copy-start(f32[1,14,64,128]{3,2,1,0:T(8,128)} %param.12) | copy-start | bytes 1376260
  16.0 53.7 %all-to-all-start = ((f32[16,2,16384]{2,1,0:T(2,128)}), f32[16,2,16384]{2,1,0:T(2,128)}, u32[]{:S(2)}, u32[]{:S(2)}) async-start(f32[16,2,16384]{2,1,0:T(2,128)} %all_to_all.8), calls=%async_computation | async-start | bytes 4194304 | tf_op jit(solution)/shard_map/all_to_all | solution.py:203
  28.5 94.6 %copy-start.6 = (f32[1,14,64,128]{3,1,2,0:T(8,128)}, f32[1,14,64,128]{3,1,2,0:T(8,128)S(1)}, u32[]{:S(2)}) copy-start(f32[1,14,64,128]{3,1,2,0:T(8,128)S(1)} %copy.631) | copy-start | bytes 1376260
  66.6 6.8 %copy-start.33 = (s32[1024]{0:T(1024)}, s32[1024]{0:T(1024)S(1)}, u32[]{:S(2)}) copy-start(s32[1024]{0:T(1024)S(1)} %pad_clamp_fusion.1) | copy-start | bytes 12292
  67.8 5.6 %copy-start.35 = (s32[1024]{0:T(1024)}, s32[1024]{0:T(1024)S(1)}, u32[]{:S(2)}) copy-start(s32[1024]{0:T(1024)S(1)} %pad_clamp_fusion.2) | copy-start | bytes 12292
  76.5 1.4 copy-start.27
  95.4 0.7 copy-start.34
  95.4 1.3 copy-start.36
  95.4 1.8 copy-start.32
  95.5 22.2 %copy-start.38 = (s32[112]{0:T(128)S(1)}, s32[112]{0:T(128)}, u32[]{:S(2)}) copy-start(s32[112]{0:T(128)} %compare_select_fusion) | copy-start | bytes 1348
  97.4 21.3 %collective-permute-start.1 = (f32[1,16,388]{2,1,0:T(8,128)S(1)}, f32[1,16,388]{2,1,0:T(8,128)S(1)}, u32[]{:S(2)}, u32[]{:S(2)}) collective-permute-start(f32[1,16,388]{2,1,0:T(8,128)S(1)} %get-tuple-element.140), channel_id=1, source_target_pairs={{16,0},{32,16},{48,32},{64,48},{80,64},{96,80},{112,96},{17,1},{33... | collective-permute-start | bytes 74504 | tf_op jit(solution)/shard_map/ppermute | solution.py:33
  110.0 8.7 %collective-permute-start.3 = (f32[1,16,388]{2,1,0:T(8,128)S(1)}, f32[1,16,388]{2,1,0:T(8,128)S(1)}, u32[]{:S(2)}, u32[]{:S(2)}) collective-permute-start(f32[1,16,388]{2,1,0:T(8,128)S(1)} %get-tuple-element.141), channel_id=1, source_target_pairs={{16,0},{32,16},{48,32},{64,48},{80,64},{96,80},{112,96},{17,1},{33... | collective-permute-start | bytes 74504 | tf_op jit(solution)/shard_map/ppermute | solution.py:33
  112.0 6.7 %collective-permute-start = (f32[1,16,388]{2,1,0:T(8,128)S(1)}, f32[1,16,388]{2,1,0:T(8,128)S(1)}, u32[]{:S(2)}, u32[]{:S(2)}) collective-permute-start(f32[1,16,388]{2,1,0:T(8,128)S(1)} %get-tuple-element.138), channel_id=1, source_target_pairs={{0,16},{16,32},{32,48},{48,64},{64,80},{80,96},{96,112},{1,17},{17... | collective-permute-start | bytes 74504 | tf_op jit(solution)/shard_map/ppermute | solution.py:32
  115.6 3.1 %collective-permute-start.2 = (f32[1,16,388]{2,1,0:T(8,128)S(1)}, f32[1,16,388]{2,1,0:T(8,128)S(1)}, u32[]{:S(2)}, u32[]{:S(2)}) collective-permute-start(f32[1,16,388]{2,1,0:T(8,128)S(1)} %get-tuple-element.139), channel_id=1, source_target_pairs={{0,16},{16,32},{32,48},{48,64},{64,80},{80,96},{96,112},{1,17},{17... | collective-permute-start | bytes 74504 | tf_op jit(solution)/shard_map/ppermute | solution.py:32
  119.6 0.7 copy-start.37
  121.7 1.4 copy-start.17
  123.1 0.8 copy-start.19
  123.9 1.0 copy-start.2
  124.9 1.0 copy-start.7
  124.9 1.2 copy-start.18
  124.9 1.4 copy-start.20
  124.9 1.5 copy-start.28
  124.9 1.6 copy-start.29
  124.9 1.7 copy-start.31
  129.5 1.2 copy-start.10
  159.7 11.4 %collective-permute-start.5 = (f32[1,16,388]{2,1,0:T(8,128)S(1)}, f32[1,16,388]{2,1,0:T(8,128)S(1)}, u32[]{:S(2)}, u32[]{:S(2)}) collective-permute-start(f32[1,16,388]{2,1,0:T(8,128)S(1)} %select_bitcast_fusion.9), channel_id=1, source_target_pairs={{16,0},{32,16},{48,32},{64,48},{80,64},{96,80},{112,96},{17,1},{33... | collective-permute-start | bytes 74504 | tf_op jit(solution)/shard_map/ppermute | solution.py:33
  167.5 4.5 %collective-permute-start.4 = (f32[1,16,388]{2,1,0:T(8,128)S(1)}, f32[1,16,388]{2,1,0:T(8,128)S(1)}, u32[]{:S(2)}, u32[]{:S(2)}) collective-permute-start(f32[1,16,388]{2,1,0:T(8,128)S(1)} %select_bitcast_fusion.10), channel_id=1, source_target_pairs={{0,16},{16,32},{32,48},{48,64},{64,80},{80,96},{96,112},{1,17},{17... | collective-permute-start | bytes 74504 | tf_op jit(solution)/shard_map/ppermute | solution.py:32
  178.4 2.9 copy-start.3
  178.4 2.9 copy-start.11
  178.4 2.9 copy-start.14
  178.4 2.9 %copy-start.23 = (f32[14,64,1]{2,0,1:T(8,128)S(1)}, f32[14,64,1]{2,0,1:T(8,128)}, u32[]{:S(2)}) copy-start(f32[14,64,1]{2,0,1:T(8,128)} %copy.544) | copy-start | bytes 10756
  178.4 2.9 %copy-start.25 = (f32[14,64,1]{2,0,1:T(8,128)S(1)}, f32[14,64,1]{2,0,1:T(8,128)}, u32[]{:S(2)}) copy-start(f32[14,64,1]{2,0,1:T(8,128)} %copy.545) | copy-start | bytes 10756
  183.4 1.2 copy-start.12
  214.0 10.9 %collective-permute-start.7 = (f32[1,16,388]{2,1,0:T(8,128)S(1)}, f32[1,16,388]{2,1,0:T(8,128)S(1)}, u32[]{:S(2)}, u32[]{:S(2)}) collective-permute-start(f32[1,16,388]{2,1,0:T(8,128)S(1)} %select_bitcast_fusion.7), channel_id=1, source_target_pairs={{16,0},{32,16},{48,32},{64,48},{80,64},{96,80},{112,96},{17,1},{33... | collective-permute-start | bytes 74504 | tf_op jit(solution)/shard_map/ppermute | solution.py:33
  219.4 6.5 %collective-permute-start.6 = (f32[1,16,388]{2,1,0:T(8,128)S(1)}, f32[1,16,388]{2,1,0:T(8,128)S(1)}, u32[]{:S(2)}, u32[]{:S(2)}) collective-permute-start(f32[1,16,388]{2,1,0:T(8,128)S(1)} %select_bitcast_fusion.8), channel_id=1, source_target_pairs={{0,16},{16,32},{32,48},{48,64},{64,80},{80,96},{96,112},{1,17},{17... | collective-permute-start | bytes 74504 | tf_op jit(solution)/shard_map/ppermute | solution.py:32
  232.2 2.9 copy-start.4
  232.2 2.9 copy-start.13
  232.2 2.9 copy-start.15
  232.2 2.9 %copy-start.24 = (f32[14,64,1]{2,0,1:T(8,128)S(1)}, f32[14,64,1]{2,0,1:T(8,128)}, u32[]{:S(2)}) copy-start(f32[14,64,1]{2,0,1:T(8,128)} %copy.560) | copy-start | bytes 10756
  232.2 2.9 %copy-start.26 = (f32[14,64,1]{2,0,1:T(8,128)S(1)}, f32[14,64,1]{2,0,1:T(8,128)}, u32[]{:S(2)}) copy-start(f32[14,64,1]{2,0,1:T(8,128)} %copy.561) | copy-start | bytes 10756
  237.2 1.2 copy-start.8
  267.9 11.1 %collective-permute-start.9 = (f32[1,16,388]{2,1,0:T(8,128)S(1)}, f32[1,16,388]{2,1,0:T(8,128)S(1)}, u32[]{:S(2)}, u32[]{:S(2)}) collective-permute-start(f32[1,16,388]{2,1,0:T(8,128)S(1)} %select_bitcast_fusion.5), channel_id=1, source_target_pairs={{16,0},{32,16},{48,32},{64,48},{80,64},{96,80},{112,96},{17,1},{33... | collective-permute-start | bytes 74504 | tf_op jit(solution)/shard_map/ppermute | solution.py:33
  272.0 8.0 %collective-permute-start.8 = (f32[1,16,388]{2,1,0:T(8,128)S(1)}, f32[1,16,388]{2,1,0:T(8,128)S(1)}, u32[]{:S(2)}, u32[]{:S(2)}) collective-permute-start(f32[1,16,388]{2,1,0:T(8,128)S(1)} %select_bitcast_fusion.6), channel_id=1, source_target_pairs={{0,16},{16,32},{32,48},{48,64},{64,80},{80,96},{96,112},{1,17},{17... | collective-permute-start | bytes 74504 | tf_op jit(solution)/shard_map/ppermute | solution.py:32
  286.3 2.9 copy-start.5
  286.3 2.9 copy-start.9
  286.3 2.9 copy-start.16
  286.3 2.9 %copy-start.21 = (f32[14,64,1]{2,0,1:T(8,128)S(1)}, f32[14,64,1]{2,0,1:T(8,128)}, u32[]{:S(2)}) copy-start(f32[14,64,1]{2,0,1:T(8,128)} %copy.576) | copy-start | bytes 10756
  286.3 2.9 %copy-start.22 = (f32[14,64,1]{2,0,1:T(8,128)S(1)}, f32[14,64,1]{2,0,1:T(8,128)}, u32[]{:S(2)}) copy-start(f32[14,64,1]{2,0,1:T(8,128)} %copy.577) | copy-start | bytes 10756
  289.2 2.9 %copy-start.1 = (s32[128,16]{0,1:T(8,128)S(1)}, s32[128,16]{0,1:T(8,128)}, u32[]{:S(2)}) copy-start(s32[128,16]{0,1:T(8,128)} %param.13) | copy-start | bytes 24580
where the time goes:
time: 294 us; the launch traced here: 292 us
  blocking collectives  113 us (38%)
  local copies, waits for them, and re-layouts  66.9 us (23%)
  starting transfers between devices  62.4 us (21%)
  other arithmetic  41.9 us (14%)
  matrix products  3.9 us (1%)
  waiting for transfers between devices  3.03 us (1%)
    all_gather x5, blocking collectives, tropic_halo(): band_table = lax.all_gather(published, 'bcol', axis=0, tiled=True)  113 us
    ppermute x5, starting transfers between devices, padded_2(): after = lax.ppermute(leading, axis, down)  31.9 us
    ppermute x5, starting transfers between devices, padded_2(): before = lax.ppermute(last, axis, up)  21.7 us
    reduce_sum x1, other arithmetic, body(): jnp.sum(jnp.where(wet_level, layer_thickness, 0.0), axis=0) / level_count  11.1 us
    concatenate x5, other arithmetic, assemble(): return jnp.concatenate([bottom_row, middle, top_row], axis=1)  10.4 us
    unnamed x123, local copies, waits for them, and re-layouts  10.2 us
    all_to_all x1, starting transfers between devices, body(): lax.all_to_all(outgoing, 'bcol', split_axis=0, concat_axis=0, tiled=True)  8.78 us
    slice x9, local copies, waits for them, and re-layouts, publish(): field[:, :, 0]  7.9 us
  transfers between devices with their start and end apart: 11, of which 3 were waited for; matrix products, arithmetic and copies ran while one was open for 3% of the time, Pallas kernels for 0%

commit v1 on v0

v1 whole, which is shorter than its diff:
```python
import functools
import math

import jax
import jax.numpy as jnp
from jax import lax
from jax.experimental import pallas as pl
from jax.experimental.pallas import tpu as pltpu
from jax.sharding import PartitionSpec as P

MESH = pl.DeviceIdType.MESH
ITERS = 4
PAIR = 2
HALO = 4
EDGE = 8
PAD = 16
CHUNK = 40
SURFACE = 0.25


def kernel(
    sizes,
    tropic_map, thickness, forcing, bottom_level, eta_prev,
    eta_next,
    forcing_v, bottom_v, prev_v,
    send_in, recv_in, send_out, recv_out,
    half, source, rhs, inverse, eta, eta_end, t_eta, t_half, rest,
    pack_src, pack_eta, col_src, col_eta,
    edge_src, edge_eta, row_src, row_eta,
    t_in, t_clinic, t_out, t_owner, owner_of,
    load_sem, prev_sem, bottom_sem,
    in_send, in_recv, out_send, out_recv,
    halo_send, halo_recv,
):
    columns, bands, block_rows, rows, levels, slots, width = sizes
    blocks = rows // block_rows
    band = lax.axis_index("brow")
    me = lax.axis_index("bcol")
    first_row = band * blocks
    base = me * slots

    pltpu.make_async_copy(eta_prev.at[0], prev_v, prev_sem).start()
    pltpu.make_async_copy(bottom_level, bottom_v, bottom_sem).start()

    def load(block):
        span = pl.ds(pl.multiple_of(block * block_rows, block_rows), block_rows)
        return pltpu.make_async_copy(
            forcing.at[:, span, :], forcing_v.at[:, span, :], load_sem.at[block]
        )

    @pl.loop(0, blocks)
    def _(block):
        load(block).start()

    def column_at(shift):
        return lax.rem(me + shift + columns, columns)

    def band_at(shift):
        return lax.rem(band + shift + bands, bands)

    barrier = pltpu.get_barrier_semaphore()

    @pl.loop(1, columns)
    def _(shift):
        pl.semaphore_signal(barrier, inc=1, device_id=(band, column_at(shift)), device_id_type=MESH)

    beside = [(up, across) for up in (-1, 1) for across in (-1, 0, 1)]
    for up, across in beside:
        pl.semaphore_signal(
            barrier, inc=1, device_id=(band_at(up), column_at(across)), device_id_type=MESH
        )

    @pl.loop(0, columns)
    def _(column):
        first, second = jnp.int32(-1), jnp.int32(-1)
        for block in reversed(range(blocks)):
            slot = tropic_map[first_row + block, column] - base
            mine = (slot >= 0) & (slot < slots)
            second = jnp.where(mine, first, second)
            first = jnp.where(mine, slot, first)
        t_in[PAIR * column] = first
        t_in[PAIR * column + 1] = second

    pltpu.make_async_copy(eta_prev.at[0], prev_v, prev_sem).wait()

    def gather_in(peer):
        for rank in range(PAIR):
            index = jnp.maximum(t_in[PAIR * peer + rank], 0)
            yield rank, prev_v[index]

    @pl.loop(1, columns)
    def _(shift):
        for rank, value in gather_in(column_at(shift)):
            send_in[PAIR * shift + rank] = value

    for rank, value in gather_in(me):
        recv_in[PAIR * me + rank] = value

    pl.semaphore_wait(barrier, columns - 1 + len(beside))

    def exchange(shift, sent, received, send_sem, recv_sem):
        peer = column_at(shift)
        return pltpu.make_async_remote_copy(
            src_ref=sent.at[pl.ds(PAIR * shift, PAIR)],
            dst_ref=received.at[pl.ds(PAIR * me, PAIR)],
            send_sem=send_sem.at[shift],
            recv_sem=recv_sem.at[shift],
            device_id=(band, peer),
            device_id_type=MESH,
        )

    @pl.loop(1, columns)
    def _(shift):
        exchange(shift, send_in, recv_in, in_send, in_recv).start()

    lane = lax.broadcasted_iota(jnp.int32, (block_rows, width), 1)
    group = lane // HALO
    pltpu.make_async_copy(bottom_level, bottom_v, bottom_sem).wait()
    pack_src[...] = jnp.zeros_like(pack_src)

    @pl.loop(0, blocks)
    def _(block):
        load(block).wait()
        start = pl.multiple_of(block * block_rows, block_rows)
        span = pl.ds(start, block_rows)
        bottom = bottom_v[span, :]

        def level(number, carry):
            depth_sum, source_sum = carry
            for step in range(2):
                k = number * 2 + step
                layer = forcing_v[k, span, :].astype(jnp.float32)
                thick = jnp.where(bottom > k, thickness[k], 0.0)
                depth_sum = depth_sum + thick
                source_sum = source_sum + thick * layer
            return depth_sum, source_sum

        zero = jnp.zeros((block_rows, width), jnp.float32)
        depth_sum, source_sum = lax.fori_loop(0, levels // 2, level, (zero, zero))
        wet = jnp.where(tropic_map[first_row + block, me] >= 0, 1.0, 0.0)
        half_depth = depth_sum * (wet * (0.5 / levels))
        src = source_sum * (wet * (1.0 / math.sqrt(levels)))
        here = pl.ds(pl.multiple_of(EDGE + start, EDGE), block_rows)
        half[0, here, :] = half_depth
        source[0, here, :] = src
        for side, turn in ((0, 0), (1, HALO)):
            moved_half = pltpu.roll(half_depth, HALO * block + turn, 1)
            moved_src = pltpu.roll(src, HALO * block + turn + width // 2, 1)
            packed = pack_src[side]
            packed = jnp.where(group == block, moved_half, packed)
            packed = jnp.where(group == block + width // 2 // HALO, moved_src, packed)
            pack_src[side] = packed

    edge_src[0, 0] = half[0, pl.ds(EDGE, EDGE), :]
    edge_src[0, 1] = source[0, pl.ds(EDGE, EDGE), :]
    edge_src[1, 0] = half[0, pl.ds(rows, EDGE), :]
    edge_src[1, 1] = source[0, pl.ds(rows, EDGE), :]

    def halo_copies(stage, pack, col, edge, row):
        copies = []
        for side, across in ((0, -1), (1, 1)):
            number = 8 * stage + side
            copies.append(
                pltpu.make_async_remote_copy(
                    src_ref=pack.at[side],
                    dst_ref=col.at[side],
                    send_sem=halo_send.at[number],
                    recv_sem=halo_recv.at[number],
                    device_id=(band, column_at(across)),
                    device_id_type=MESH,
                )
            )
        for place, (up, across) in enumerate(beside):
            number = 8 * stage + 2 + place
            copies.append(
                pltpu.make_async_remote_copy(
                    src_ref=edge.at[0 if up < 0 else 1],
                    dst_ref=row.at[place],
                    send_sem=halo_send.at[number],
                    recv_sem=halo_recv.at[number],
                    device_id=(band_at(up), column_at(across)),
                    device_id_type=MESH,
                )
            )
        return copies

    first_halos = halo_copies(0, pack_src, col_src, edge_src, row_src)
    for copy in first_halos:
        copy.start()

    for block in range(blocks):
        value = tropic_map[first_row + block, me]
        owner_of[block] = jnp.where(value >= 0, value // slots, -1)
    for block in range(blocks):
        owner = owner_of[block]
        rank = jnp.int32(0)
        for before in range(block):
            rank = jnp.where(owner_of[before] == owner, 1, rank)
        t_clinic[block] = jnp.where(owner >= 0, owner * PAIR + rank, 0)

    @pl.loop(0, columns)
    def _(owner):
        first, second = jnp.int32(0), jnp.int32(0)
        for block in reversed(range(blocks)):
            mine = owner_of[block] == owner
            second = jnp.where(mine, first, second)
            first = jnp.where(mine, block, first)
        t_out[PAIR * owner] = first
        t_out[PAIR * owner + 1] = second

    @pl.loop(0, slots)
    def _(slot):
        place = jnp.int32(0)
        for entry in range(PAIR * columns):
            place = jnp.where(t_in[entry] == slot, entry, place)
        t_owner[slot] = place

    for copy in first_halos:
        copy.wait()

    has_above = jnp.where(band > 0, 1.0, 0.0)
    has_below = jnp.where(band < bands - 1, 1.0, 0.0)
    edge_lane = lax.broadcasted_iota(jnp.int32, (EDGE, width), 1) < width // 2
    edges = (
        (0, 3, has_above),
        (EDGE + rows, 0, has_below),
    )

    def edge_rows(field, arrived):
        for at, place, inside in edges:
            there = pl.ds(at, EDGE)
            right, middle, left = (arrived(place + k) for k in range(3))
            field[0, there, :] = middle * inside
            field[1, there, :] = jnp.where(edge_lane, right, left) * inside

    edge_rows(half, lambda place: row_src[place, 0])
    edge_rows(source, lambda place: row_src[place, 1])

    right_half = lane < width // 2

    @pl.loop(0, blocks)
    def _(block):
        here = pl.ds(pl.multiple_of(EDGE + block * block_rows, EDGE), block_rows)
        for field, turn in ((half, 0), (source, width // 2)):
            from_right = pltpu.roll(col_src[0], 2 * width - HALO * block - turn, 1)
            from_left = pltpu.roll(col_src[1], 2 * width - HALO * (block + 1) - turn, 1)
            field[1, here, :] = jnp.where(right_half, from_right, from_left)

    total_rows = rows + 2 * EDGE
    chunk_lane = lax.broadcasted_iota(jnp.int32, (CHUNK, width), 1)

    def beside_sum(main, side):
        at_end, at_start = chunk_lane == width - 1, chunk_lane == 0
        main_sum = pltpu.roll(jnp.where(at_end, side, main), 1, 1) + pltpu.roll(
            jnp.where(at_start, side, main), width - 1, 1
        )
        side_sum = pltpu.roll(jnp.where(at_end, main, side), 1, 1) + pltpu.roll(
            jnp.where(at_start, main, side), width - 1, 1
        )
        return main_sum, side_sum

    @pl.loop(0, total_rows // CHUNK)
    def _(chunk):
        start = pl.multiple_of(chunk * CHUNK, EDGE)
        here, there = pl.ds(start, CHUNK), pl.ds(pl.multiple_of(start + EDGE, EDGE), CHUNK)
        sums = beside_sum(half[0, here, :], half[1, here, :])
        for part in range(2):
            value = half[part, here, :]
            t_half[part, there, :] = value + 0.5 * sums[part]
            rest[part, here, :] = (SURFACE + 8.0 * value) + sums[part]

    @pl.loop(0, total_rows // CHUNK)
    def _(chunk):
        start = pl.multiple_of(chunk * CHUNK, EDGE)
        here = pl.ds(start, CHUNK)
        above, below = pl.ds(start + EDGE - 1, CHUNK), pl.ds(start + EDGE + 1, CHUNK)
        for part in range(2):
            total = rest[part, here, :] + (t_half[part, above, :] + t_half[part, below, :])
            inverse[part, here, :] = 1.0 / total

    right_column, left_column = column_at(1), column_at(-1)

    def wet_of(row, column):
        return jnp.where(tropic_map[row, column] >= 0, 1.0, 0.0)

    @pl.loop(0, blocks)
    def _(block):
        here = pl.ds(pl.multiple_of(EDGE + block * block_rows, EDGE), block_rows)
        row = first_row + block
        inverse[0, here, :] = inverse[0, here, :] * wet_of(row, me)
        inverse[1, here, :] = inverse[1, here, :] * jnp.where(
            right_half, wet_of(row, right_column), wet_of(row, left_column)
        )

    above_row = jnp.maximum(first_row - 1, 0)
    below_row = jnp.minimum(first_row + blocks, bands * blocks - 1)
    for (at, _, inside), row in zip(edges, (above_row, below_row)):
        there = pl.ds(at, EDGE)
        inverse[0, there, :] = inverse[0, there, :] * (wet_of(row, me) * inside)
        inverse[1, there, :] = inverse[1, there, :] * (
            jnp.where(edge_lane, wet_of(row, right_column), wet_of(row, left_column)) * inside
        )

    @pl.loop(1, columns)
    def _(shift):
        exchange(shift, send_in, recv_in, in_send, in_recv).wait()

    pack_eta[...] = jnp.zeros_like(pack_eta)

    @pl.loop(0, blocks)
    def _(block):
        here = pl.ds(pl.multiple_of(EDGE + block * block_rows, EDGE), block_rows)
        value = recv_in[t_clinic[block]] * wet_of(first_row + block, me)
        eta[0, here, :] = value
        first = pltpu.roll(value, HALO * block, 1)
        last = pltpu.roll(value, HALO * block + HALO + width // 2, 1)
        packed = pack_eta[0]
        packed = jnp.where(group == block, first, packed)
        packed = jnp.where(group == block + width // 2 // HALO, last, packed)
        pack_eta[0] = packed

    pack_eta[1] = pack_eta[0]
    edge_eta[0] = eta[0, pl.ds(EDGE, EDGE), :]
    edge_eta[1] = eta[0, pl.ds(rows, EDGE), :]
    second_halos = halo_copies(1, pack_eta, col_eta, edge_eta, row_eta)
    for copy in second_halos:
        copy.start()
    for copy in second_halos:
        copy.wait()

    edge_rows(eta, lambda place: row_eta[place])

    @pl.loop(0, blocks)
    def _(block):
        here = pl.ds(pl.multiple_of(EDGE + block * block_rows, EDGE), block_rows)
        from_right = pltpu.roll(col_eta[0], 2 * width - HALO * block, 1)
        from_left = pltpu.roll(col_eta[1], 2 * width - HALO * (block + 1) - width // 2, 1)
        eta[1, here, :] = jnp.where(right_half, from_right, from_left)

    @pl.loop(0, total_rows // CHUNK)
    def _(chunk):
        here = pl.ds(pl.multiple_of(chunk * CHUNK, EDGE), CHUNK)
        for part in range(2):
            rhs[part, here, :] = (SURFACE + 2.0 * half[part, here, :]) * eta[
                part, here, :
            ] + source[part, here, :]

    def spread():
        @pl.loop(0, total_rows // CHUNK)
        def _(chunk):
            start = pl.multiple_of(chunk * CHUNK, EDGE)
            here, there = pl.ds(start, CHUNK), pl.ds(pl.multiple_of(start + EDGE, EDGE), CHUNK)
            values = [eta[part, here, :] for part in range(2)]
            halves = [half[part, here, :] for part in range(2)]
            scaled = [value * weight for value, weight in zip(values, halves)]
            sums = beside_sum(*values)
            scaled_sums = beside_sum(*scaled)
            for part in range(2):
                t_eta[part, there, :] = values[part] + 0.5 * sums[part]
                t_half[part, there, :] = scaled[part] + 0.5 * scaled_sums[part]
                rest[part, here, :] = (
                    rhs[part, here, :] + halves[part] * sums[part] + scaled_sums[part]
                )

    def settle(part, start, count):
        here = pl.ds(start, count)
        above, below = pl.ds(start + EDGE - 1, count), pl.ds(start + EDGE + 1, count)
        total = rest[part, here, :] + (t_half[part, above, :] + t_half[part, below, :])
        total = total + half[part, here, :] * (t_eta[part, above, :] + t_eta[part, below, :])
        return total * inverse[part, here, :]

    @pl.loop(0, ITERS - 1)
    def _(iteration):
        spread()

        @pl.loop(0, total_rows // CHUNK)
        def _(chunk):
            start = pl.multiple_of(chunk * CHUNK, EDGE)
            for part in range(2):
                eta[part, pl.ds(start, CHUNK), :] = settle(part, start, CHUNK)

    spread()

    @pl.loop(0, blocks)
    def _(block):
        start = pl.multiple_of(EDGE + block * block_rows, EDGE)
        eta_end[block] = settle(0, start, block_rows)

    @pl.loop(1, columns)
    def _(shift):
        peer = column_at(shift)
        for rank in range(PAIR):
            send_out[PAIR * shift + rank] = eta_end[t_out[PAIR * peer + rank]]
        exchange(shift, send_out, recv_out, out_send, out_recv).start()

    for rank in range(PAIR):
        recv_out[PAIR * me + rank] = eta_end[t_out[PAIR * me + rank]]

    @pl.loop(1, columns)
    def _(shift):
        exchange(shift, send_out, recv_out, out_send, out_recv).wait()

    @pl.loop(0, slots)
    def _(slot):
        eta_next[0, slot] = recv_out[t_owner[slot]]


def solution(mesh):
    columns, bands = mesh.shape["bcol"], mesh.shape["brow"]

    def body(forcing, bottom_level, thickness, eta_prev, tropic_map):
        levels, rows, width = forcing.shape
        slots, block_rows = eta_prev.shape[1], eta_prev.shape[2]
        blocks = rows // block_rows
        sizes = (columns, bands, block_rows, rows, levels, slots, width)
        f32 = jnp.float32
        padded, more = rows + 2 * EDGE, rows + 2 * PAD
        dma = pltpu.SemaphoreType.DMA
        scratch = [
            pltpu.VMEM(forcing.shape, forcing.dtype),
            pltpu.VMEM((rows, width), jnp.int32),
            pltpu.VMEM((slots, block_rows, width), f32),
        ]
        scratch += [pltpu.VMEM((PAIR * columns, block_rows, width), f32)] * 4
        scratch += [pltpu.VMEM((2, padded, width), f32)] * 5
        scratch += [pltpu.VMEM((blocks, block_rows, width), f32)]
        scratch += [pltpu.VMEM((2, more, width), f32)] * 2
        scratch += [pltpu.VMEM((2, padded, width), f32)]
        scratch += [pltpu.VMEM((2, block_rows, width), f32)] * 4
        scratch += [pltpu.VMEM((2, 2, EDGE, width), f32), pltpu.VMEM((2, EDGE, width), f32)]
        scratch += [pltpu.VMEM((6, 2, EDGE, width), f32), pltpu.VMEM((6, EDGE, width), f32)]
        scratch += [
            pltpu.SMEM((count,), jnp.int32)
            for count in (PAIR * columns, blocks, PAIR * columns, slots, blocks)
        ]
        scratch += [dma((blocks,)), dma, dma]
        scratch += [dma((columns,))] * 4
        scratch += [dma((16,))] * 2
        hbm = pl.BlockSpec(memory_space=pl.ANY)
        smem = pl.BlockSpec(memory_space=pltpu.SMEM)
        return pl.pallas_call(
            functools.partial(kernel, sizes),
            out_shape=jax.ShapeDtypeStruct(eta_prev.shape, f32),
            in_specs=[smem, smem, hbm, hbm, hbm],
            out_specs=pl.BlockSpec(memory_space=pltpu.VMEM),
            scratch_shapes=scratch,
            compiler_params=pltpu.CompilerParams(
                collective_id=0, has_side_effects=True, vmem_limit_bytes=56 * 1024 * 1024
            ),
            cost_estimate=pl.CostEstimate(
                flops=60_000_000, bytes_accessed=18_000_000, transcendentals=0
            ),
        )(tropic_map, thickness, forcing, bottom_level, eta_prev)

    in_specs = (P(None, "brow", "bcol"), P("brow", "bcol"), P(), P("brow", "bcol", None, None), P())
    out_specs = P("brow", "bcol", None, None)
    return jax.shard_map(body, mesh=mesh, in_specs=in_specs, out_specs=out_specs, check_vma=False)
```

time: 294 us -> 71.9 us (0.24)
  blocking collectives: 113 us -> 0 us
  Pallas kernels: 0 us -> 68.4 us
  local copies, waits for them, and re-layouts: 66.9 us -> 3.25 us
  starting transfers between devices: 62.4 us -> 0 us
  other arithmetic: 41.9 us -> 0 us
  matrix products: 3.9 us -> 0 us
  waiting for transfers between devices: 3.03 us -> 0 us
    all_gather x5 -> x0, blocking collectives: 113 us -> none  [tropic_halo(): band_table = lax.all_gather(published, 'bcol', axis=0, tiled=True)]
    pallas_call x0 -> x1, Pallas kernels: none -> 68.4 us  [body(): pl.pallas_call(functools.partial(kernel, sizes), out_shape=jax.ShapeDtype...]
    ppermute x10 -> x0, starting transfers between devices: 53.6 us -> none  [the longest x5 31.9 us: padded_2(): after = lax.ppermute(leading, axis, down)]
    gather x15 -> x0, local copies, waits for them, and re-layouts: 19.7 us -> none  [the longest x5 7.1 us: tropic_halo(): jnp.take(table, neighbour_index, axis=0).reshape(slot_count, 8, rim_width)]
    concatenate x9 -> x0, other arithmetic: 16.4 us -> none  [the longest x5 10.4 us: assemble(): return jnp.concatenate([bottom_row, middle, top_row], axis=1)]
    reduce_sum x5 -> x0, other arithmetic: 14.2 us -> none  [the longest x1 11.1 us: body(): jnp.sum(jnp.where(wet_level, layer_thickness, 0.0), axis=0) / level_count]
    slice x25 -> x0, local copies, waits for them, and re-layouts: 12.8 us -> none  [the longest x9 7.9 us: publish(): field[:, :, 0]]
    another operation x17 -> x0, local copies, waits for them, and re-layouts: 8.95 us -> none  [the longest x5 4.57 us: assemble(): right_side[:, :, None]]
  transfers between devices with their start and end apart: 11 -> 0, of which waited for: 3 -> 0; matrix products, arithmetic and copies ran while one was open for 3% -> 0% of each run, Pallas kernels for 0% -> 0%
where the time goes in v1:
time: 71.9 us; the launch traced here: 71.6 us
  Pallas kernels  68.4 us (95%)
  local copies, waits for them, and re-layouts  3.25 us (5%)
    pallas_call x1, Pallas kernels, body(): pl.pallas_call(functools.partial(kernel, sizes), out_shape=jax.ShapeDtype...  68.4 us
    unnamed x2, local copies, waits for them, and re-layouts  3.25 us

profile of v1, /device:TPU:1, one launch (start us, length us, event | category | flops | bytes accessed | tf_op | source)
XLA Modules:
  0.0 71.6 jit_solution(5883792016714544931)
XLA Ops:
  0.0 1.4 %copy.6.tropic_map = s32[128,16]{1,0:T(8,128)} copy(s32[128,16]{0,1:T(8,128)} %param.9) | data formatting | bytes 16384 | tf_op args[4]
  1.4 68.4 %shard_map.55 = f32[1,14,64,128]{3,2,1,0:T(8,128)} custom-call(s32[128,16]{1,0:T(8,128)} %copy.6.tropic_map, f32[62]{0:T(128)} %thickness.1, bf16[62,1024,128]{2,1,0:T(8,128)(2,1)} %forcing.1, s32[1024,128]{1,0:T(8,128)} %bottom_level.1, f32[1,14,64,128]{3,2,1,0:T(8,128)} %eta_prev.1), custom_call_target="tpu_custom_call" | custom-call | flops 60000000 | bytes 18000000 | tf_op jit(solution)/shard_map/pallas_call | solution.py:441
  69.8 1.8 %copy.8 = f32[1,14,64,128]{3,2,1,0:T(8,128)} copy(f32[1,14,64,128]{3,2,1,0:T(8,128)} %shard_map.55) | data formatting | bytes 917504

commit v2 on v1

v2 whole, which is shorter than its diff:
```python
import functools
import math

import jax
import jax.numpy as jnp
from jax import lax
from jax.experimental import pallas as pl
from jax.experimental.pallas import tpu as pltpu
from jax.sharding import PartitionSpec as P

MESH = pl.DeviceIdType.MESH
ITERS = 4
PAIR = 2
HALO = 4
TILE = 8
FINE = 9
SURFACE = 0.25


def kernel(
    sizes,
    tropic_map, thickness, forcing, bottom_level, eta_prev,
    eta_next,
    forcing_v, bottom_v, prev_v,
    send_in, recv_in, send_out, recv_out, eta_end,
    nat_half, nat_source, nat_eta, corner,
    raw, half, source, rhs, inverse, eta, rest,
    g_eta, g_half,
    strip_first, strip_eta, col_first, col_eta,
    edge_first, row_first, row_eta,
    map_v, thick,
    t_in, t_clinic, t_out, t_owner, owner_of,
    load_sem, prev_sem, bottom_sem, map_sem, thick_sem,
    in_send, in_recv, out_send, out_recv,
    halo_send, halo_recv,
):
    columns, bands, block_rows, rows, levels, slots, width = sizes
    blocks = rows // block_rows
    band = lax.axis_index("brow")
    me = lax.axis_index("bcol")
    base = me * slots
    first_row = band * blocks

    def column_at(shift):
        return lax.rem(me + shift + columns, columns)

    def band_at(shift):
        return lax.rem(band + shift + bands, bands)

    barrier = pltpu.get_barrier_semaphore()

    @pl.loop(1, columns)
    def _(shift):
        pl.semaphore_signal(barrier, inc=1, device_id=(band, column_at(shift)), device_id_type=MESH)

    beside = [(up, across) for up in (-1, 1) for across in (-1, 0, 1)]
    for up, across in beside:
        pl.semaphore_signal(
            barrier, inc=1, device_id=(band_at(up), column_at(across)), device_id_type=MESH
        )

    map_copy = pltpu.make_async_copy(tropic_map, map_v, map_sem)
    prev_copy = pltpu.make_async_copy(eta_prev.at[0], prev_v, prev_sem)
    thick_copy = pltpu.make_async_copy(thickness, thick, thick_sem)
    bottom_copy = pltpu.make_async_copy(bottom_level, bottom_v, bottom_sem)
    for copy in (map_copy, prev_copy, thick_copy, bottom_copy):
        copy.start()

    def load(block):
        span = pl.ds(pl.multiple_of(block * block_rows, block_rows), block_rows)
        return pltpu.make_async_copy(
            forcing.at[:, span, :], forcing_v.at[:, span, :], load_sem.at[block]
        )

    @pl.loop(0, blocks)
    def _(block):
        load(block).start()

    map_copy.wait()

    @pl.loop(0, columns)
    def _(column):
        first, second = jnp.int32(-1), jnp.int32(-1)
        for block in reversed(range(blocks)):
            slot = map_v[column, first_row + block] - base
            mine = (slot >= 0) & (slot < slots)
            second = jnp.where(mine, first, second)
            first = jnp.where(mine, slot, first)
        t_in[PAIR * column] = first
        t_in[PAIR * column + 1] = second

    prev_copy.wait()

    def gather_in(peer):
        for rank in range(PAIR):
            index = jnp.maximum(t_in[PAIR * peer + rank], 0)
            yield rank, prev_v[index]

    @pl.loop(1, columns)
    def _(shift):
        for rank, value in gather_in(column_at(shift)):
            send_in[PAIR * shift + rank] = value

    for rank, value in gather_in(me):
        recv_in[PAIR * me + rank] = value

    pl.semaphore_wait(barrier, columns - 1 + len(beside))

    def exchange(shift, sent, received, send_sem, recv_sem):
        peer = column_at(shift)
        return pltpu.make_async_remote_copy(
            src_ref=sent.at[pl.ds(PAIR * shift, PAIR)],
            dst_ref=received.at[pl.ds(PAIR * me, PAIR)],
            send_sem=send_sem.at[shift],
            recv_sem=recv_sem.at[shift],
            device_id=(band, peer),
            device_id_type=MESH,
        )

    @pl.loop(1, columns)
    def _(shift):
        exchange(shift, send_in, recv_in, in_send, in_recv).start()

    thick_copy.wait()
    bottom_copy.wait()

    @pl.loop(0, blocks)
    def _(block):
        load(block).wait()
        start = pl.multiple_of(block * block_rows, block_rows)
        span = pl.ds(start, block_rows)
        bottom = bottom_v[span, :]

        def level(number, carry):
            depth_sum, source_sum = carry
            for step in range(2):
                k = number * 2 + step
                layer = forcing_v[k, span, :].astype(jnp.float32)
                weight = jnp.where(bottom > k, thick[k], 0.0)
                depth_sum = depth_sum + weight
                source_sum = source_sum + weight * layer
            return depth_sum, source_sum

        zero = jnp.zeros((block_rows, width), jnp.float32)
        depth_sum, source_sum = lax.fori_loop(0, levels // 2, level, (zero, zero))
        wet = jnp.where(map_v[me, first_row + block] >= 0, 1.0, 0.0)
        here = pl.ds(pl.multiple_of(TILE + start, TILE), block_rows)
        nat_half[here, :] = depth_sum * (wet * (0.5 / levels)) + (wet - 1.0)
        nat_source[here, :] = source_sum * (wet * (1.0 / math.sqrt(levels)))

    def remote(number, src, dst, device):
        return pltpu.make_async_remote_copy(
            src_ref=src,
            dst_ref=dst,
            send_sem=halo_send.at[number],
            recv_sem=halo_recv.at[number],
            device_id=device,
            device_id_type=MESH,
        )

    def row_copies(stage, top, bottom, row):
        return [
            remote(
                8 * stage + 2 + place,
                top if up < 0 else bottom,
                row.at[place],
                (band_at(up), column_at(across)),
            )
            for place, (up, across) in enumerate(beside)
        ]

    def col_copies(stage, strip, col):
        return [
            remote(8 * stage + side, strip, col.at[side], (band, column_at(across)))
            for side, across in ((0, -1), (1, 1))
        ]

    has_above = jnp.where(band > 0, 1.0, 0.0)
    has_below = jnp.where(band < bands - 1, 1.0, 0.0)
    tile_lane = lax.broadcasted_iota(jnp.int32, (TILE, width), 1)
    low_lane = tile_lane < width // 2
    low_row = lax.broadcasted_iota(jnp.int32, (TILE, width), 0) < HALO
    low_rows = lax.broadcasted_iota(jnp.int32, (FINE, TILE, width), 1) < HALO
    above_at, below_at = 0, TILE + rows
    near = [(n, n) for n in range(TILE - HALO, TILE)]
    near += [(below_at + m, TILE + m) for m in range(HALO)]
    fine_near = sorted({n % FINE for n, _ in near})
    last = width - TILE
    side_rows = pl.ds(width, TILE)

    def turn(nat, field, fine):
        for f in fine:
            field[f, pl.ds(0, width), :] = nat[pl.ds(f, width, stride=FINE), :].T

    def strip_of(field):
        return jnp.where(low_rows, field[:, pl.ds(0, TILE), :], field[:, pl.ds(last, TILE), :])

    def fill(nat, field, arrived_row, arrived_col, outside):
        for at, place, inside in ((above_at, 3, has_above), (below_at, 0, has_below)):
            right, middle, left = (arrived_row(place + k) for k in range(3))
            absent = (1.0 - inside) * outside
            nat[pl.ds(at, TILE), :] = middle * inside + absent
            side = jnp.where(low_lane, right, left) * inside + absent
            corner[pl.ds(TILE if at else 0, TILE), :] = side
        turn(nat, field, fine_near)
        turned = corner[...].T
        sides = jnp.where(low_row, turned[0:TILE, :], turned[last:width, :])
        field[:, side_rows, :] = jnp.where(low_rows, arrived_col(0), arrived_col(1))
        for n, lane in near:
            f, to = n % FINE, n // FINE
            moved = pltpu.roll(sides, (to - lane) % width, 1)
            field[f, side_rows, :] = jnp.where(tile_lane == to, moved, field[f, side_rows, :])

    corner[...] = jnp.zeros_like(corner)
    for number, nat in enumerate((nat_half, nat_source)):
        edge_first[0, number] = nat[pl.ds(TILE, TILE), :]
        edge_first[1, number] = nat[pl.ds(rows, TILE), :]
    first_rows = row_copies(0, edge_first.at[0], edge_first.at[1], row_first)
    for copy in first_rows:
        copy.start()
    turn(nat_half, raw, range(FINE))
    turn(nat_source, source, range(FINE))
    strip_first[0] = strip_of(raw)
    strip_first[1] = strip_of(source)
    first_cols = col_copies(0, strip_first, col_first)
    for copy in first_cols:
        copy.start()

    for block in range(blocks):
        value = map_v[me, first_row + block]
        owner_of[block] = jnp.where(value >= 0, value // slots, -1)
    for block in range(blocks):
        owner = owner_of[block]
        rank = jnp.int32(0)
        for before in range(block):
            rank = jnp.where(owner_of[before] == owner, 1, rank)
        t_clinic[block] = jnp.where(owner >= 0, owner * PAIR + rank, 0)

    @pl.loop(0, columns)
    def _(owner):
        first, second = jnp.int32(0), jnp.int32(0)
        for block in reversed(range(blocks)):
            mine = owner_of[block] == owner
            second = jnp.where(mine, first, second)
            first = jnp.where(mine, block, first)
        t_out[PAIR * owner] = first
        t_out[PAIR * owner + 1] = second

    @pl.loop(0, slots)
    def _(slot):
        place = jnp.int32(0)
        for entry in range(PAIR * columns):
            place = jnp.where(t_in[entry] == slot, entry, place)
        t_owner[slot] = place

    for copy in first_rows + first_cols:
        copy.wait()
    fill(nat_half, raw, lambda p: row_first[p, 0], lambda s: col_first[s, 0], -1.0)
    fill(nat_source, source, lambda p: row_first[p, 1], lambda s: col_first[s, 1], 0.0)

    tiles = width // TILE + 1

    def tile_at(tile):
        return pl.ds(TILE * tile, TILE)

    def row_sum(value):
        before = jnp.concatenate([pltpu.roll(value[FINE - 1 :], 1, 2), value[: FINE - 1]], axis=0)
        after = jnp.concatenate([value[1:], pltpu.roll(value[:1], width - 1, 2)], axis=0)
        return before + after

    def put(field, tile, value):
        field[:, tile_at(tile + 1), :] = value
        if tile == tiles - 1:
            field[:, tile_at(0), :] = value
        if tile == 0:
            field[:, tile_at(tiles + 1), :] = value

    def col_sum(field, tile):
        start = TILE * (tile + 1)
        return field[:, pl.ds(start - 1, TILE), :] + field[:, pl.ds(start + 1, TILE), :]

    for tile in range(tiles):
        value = jnp.maximum(raw[:, tile_at(tile), :], 0.0)
        half[:, tile_at(tile), :] = value
        around = row_sum(value)
        put(g_half, tile, value + 0.5 * around)
        rest[:, tile_at(tile), :] = (SURFACE + 8.0 * value) + around
    for tile in range(tiles):
        diagonal = rest[:, tile_at(tile), :] + col_sum(g_half, tile)
        wet = raw[:, tile_at(tile), :] >= 0.0
        inverse[:, tile_at(tile), :] = jnp.where(wet, 1.0 / diagonal, 0.0)

    @pl.loop(1, columns)
    def _(shift):
        exchange(shift, send_in, recv_in, in_send, in_recv).wait()

    for block in range(blocks):
        wet = jnp.where(map_v[me, first_row + block] >= 0, 1.0, 0.0)
        nat_eta[pl.ds(TILE + block * block_rows, block_rows), :] = recv_in[t_clinic[block]] * wet

    second_rows = row_copies(
        1, nat_eta.at[pl.ds(TILE, TILE)], nat_eta.at[pl.ds(rows, TILE)], row_eta
    )
    for copy in second_rows:
        copy.start()
    turn(nat_eta, eta, range(FINE))
    strip_eta[...] = strip_of(eta)
    second_cols = col_copies(1, strip_eta, col_eta)
    for copy in second_cols:
        copy.start()
    for copy in second_rows + second_cols:
        copy.wait()
    fill(nat_eta, eta, lambda p: row_eta[p], lambda s: col_eta[s], 0.0)
    for tile in range(tiles):
        here = tile_at(tile)
        rhs[:, here, :] = (SURFACE + 2.0 * half[:, here, :]) * eta[:, here, :] + source[:, here, :]

    @pl.loop(0, ITERS)
    def _(iteration):
        for tile in range(tiles):
            here = tile_at(tile)
            value, weight = eta[:, here, :], half[:, here, :]
            scaled = value * weight
            around, scaled_around = row_sum(value), row_sum(scaled)
            put(g_eta, tile, value + 0.5 * around)
            put(g_half, tile, scaled + 0.5 * scaled_around)
            rest[:, here, :] = rhs[:, here, :] + weight * around + scaled_around
        for tile in range(tiles):
            here = tile_at(tile)
            total = rest[:, here, :] + col_sum(g_half, tile)
            total = total + half[:, here, :] * col_sum(g_eta, tile)
            eta[:, here, :] = total * inverse[:, here, :]

    for f in range(FINE):
        nat_half[pl.ds(f, width, stride=FINE), :] = eta[f, pl.ds(0, width), :].T
    for block in range(blocks):
        eta_end[block] = nat_half[pl.ds(TILE + block * block_rows, block_rows), :]

    @pl.loop(1, columns)
    def _(shift):
        peer = column_at(shift)
        for rank in range(PAIR):
            send_out[PAIR * shift + rank] = eta_end[t_out[PAIR * peer + rank]]
        exchange(shift, send_out, recv_out, out_send, out_recv).start()

    for rank in range(PAIR):
        recv_out[PAIR * me + rank] = eta_end[t_out[PAIR * me + rank]]

    @pl.loop(1, columns)
    def _(shift):
        exchange(shift, send_out, recv_out, out_send, out_recv).wait()

    @pl.loop(0, slots)
    def _(slot):
        eta_next[0, slot] = recv_out[t_owner[slot]]


def solution(mesh):
    columns, bands = mesh.shape["bcol"], mesh.shape["brow"]

    def body(forcing, bottom_level, thickness, eta_prev, tropic_map):
        levels, rows, width = forcing.shape
        slots, block_rows = eta_prev.shape[1], eta_prev.shape[2]
        blocks = rows // block_rows
        sizes = (columns, bands, block_rows, rows, levels, slots, width)
        f32, dma = jnp.float32, pltpu.SemaphoreType.DMA

        def vmem(*shape):
            return pltpu.VMEM(shape, f32)

        def smem(*shape):
            return pltpu.SMEM(shape, jnp.int32)

        tall = width + TILE
        scratch = [
            pltpu.VMEM(forcing.shape, forcing.dtype),
            pltpu.VMEM((rows, width), jnp.int32),
            vmem(slots, block_rows, width),
        ]
        scratch += [vmem(PAIR * columns, block_rows, width)] * 4
        scratch += [vmem(blocks, block_rows, width)]
        scratch += [vmem(FINE * width, width)] * 3 + [vmem(width, width)]
        scratch += [vmem(FINE, tall, width)] * 7
        scratch += [vmem(FINE, tall + 2 * TILE, width)] * 2
        scratch += [vmem(2, FINE, TILE, width), vmem(FINE, TILE, width)]
        scratch += [vmem(2, 2, FINE, TILE, width), vmem(2, FINE, TILE, width)]
        scratch += [vmem(2, 2, TILE, width), vmem(6, 2, TILE, width), vmem(6, TILE, width)]
        scratch += [smem(*tropic_map.shape[::-1]), pltpu.SMEM((levels,), f32)]
        scratch += [
            smem(PAIR * columns), smem(blocks), smem(PAIR * columns), smem(slots), smem(blocks)
        ]
        scratch += [dma((blocks,))] + [dma] * 4 + [dma((columns,))] * 4 + [dma((16,))] * 2
        return pl.pallas_call(
            functools.partial(kernel, sizes),
            out_shape=jax.ShapeDtypeStruct(eta_prev.shape, f32),
            in_specs=[pl.BlockSpec(memory_space=pl.ANY)] * 5,
            out_specs=pl.BlockSpec(memory_space=pltpu.VMEM),
            scratch_shapes=scratch,
            compiler_params=pltpu.CompilerParams(
                collective_id=0, has_side_effects=True, vmem_limit_bytes=56 * 1024 * 1024
            ),
            cost_estimate=pl.CostEstimate(
                flops=60_000_000, bytes_accessed=18_000_000, transcendentals=0
            ),
        )(tropic_map.T, thickness, forcing, bottom_level, eta_prev)

    in_specs = (P(None, "brow", "bcol"), P("brow", "bcol"), P(), P("brow", "bcol", None, None), P())
    out_specs = P("brow", "bcol", None, None)
    return jax.shard_map(body, mesh=mesh, in_specs=in_specs, out_specs=out_specs, check_vma=False)
```

time: 71.9 us -> 50.5 us (0.70)
  Pallas kernels: 68.4 us -> 48.6 us
  local copies, waits for them, and re-layouts: 3.25 us -> 1.82 us
    pallas_call x1, Pallas kernels: 68.4 us -> 48.6 us  [body(): pl.pallas_call(functools.partial(kernel, sizes), out_shape=jax.ShapeDtype...]
    unnamed x2 -> x1, local copies, waits for them, and re-layouts: 3.25 us -> 1.82 us
where the time goes in v2:
time: 50.5 us; the launch traced here: 50.4 us
  Pallas kernels  48.6 us (96%)
  local copies, waits for them, and re-layouts  1.82 us (4%)
    pallas_call x1, Pallas kernels, body(): pl.pallas_call(functools.partial(kernel, sizes), out_shape=jax.ShapeDtype...  48.6 us
    unnamed x1, local copies, waits for them, and re-layouts  1.82 us

profile of v2, /device:TPU:1, one launch (start us, length us, event | category | flops | bytes accessed | tf_op | source)
XLA Modules:
  0.0 50.4 jit_solution(17785435223985515719)
XLA Ops:
  0.0 48.6 %shard_map.55 = f32[1,14,64,128]{3,2,1,0:T(8,128)} custom-call(s32[16,128]{1,0:T(8,128)} %bitcast.1, f32[62]{0:T(128)} %thickness.1, bf16[62,1024,128]{2,1,0:T(8,128)(2,1)} %forcing.1, s32[1024,128]{1,0:T(8,128)} %bottom_level.1, f32[1,14,64,128]{3,2,1,0:T(8,128)} %eta_prev.1), custom_call_target="tpu_custom_call" | custom-call | flops 60000000 | bytes 18000000 | tf_op jit(solution)/shard_map/pallas_call | solution.py:393
  48.6 1.8 %copy.7 = f32[1,14,64,128]{3,2,1,0:T(8,128)} copy(f32[1,14,64,128]{3,2,1,0:T(8,128)} %shard_map.55) | data formatting | bytes 917504

commit v3 on v2

--- a/solution.py
+++ b/solution.py
@@ -13,6 +13,9 @@
 PAIR = 2
 HALO = 4
 TILE = 8
+IN_ROWS = 40
+OUT_ROW, OUT_ROWS = 4, 32
+CHUNK = 128
 FINE = 9
 SURFACE = 0.25
 
@@ -22,16 +25,18 @@
     tropic_map, thickness, forcing, bottom_level, eta_prev,
     eta_next,
     forcing_v, bottom_v, prev_v,
-    send_in, recv_in, send_out, recv_out, eta_end,
+    send_in_a, recv_in_a, send_in_b, recv_in_b,
+    send_out_a, recv_out_a, send_out_b, recv_out_b,
+    end_a, end_b,
     nat_half, nat_source, nat_eta, corner,
-    raw, half, source, rhs, inverse, eta, rest,
+    raw, half, source, rhs, inverse, eta_a, eta_b, rest,
     g_eta, g_half,
-    strip_first, strip_eta, col_first, col_eta,
+    strip_first, col_first, strip_eta, col_eta,
     edge_first, row_first, row_eta,
     map_v, thick,
     t_in, t_clinic, t_out, t_owner, owner_of,
     load_sem, prev_sem, bottom_sem, map_sem, thick_sem,
-    in_send, in_recv, out_send, out_recv,
+    exchange_send, exchange_recv,
     halo_send, halo_recv,
 ):
     columns, bands, block_rows, rows, levels, slots, width = sizes
@@ -67,12 +72,12 @@
         copy.start()
 
     def load(block):
-        span = pl.ds(pl.multiple_of(block * block_rows, block_rows), block_rows)
+        span = pl.ds(pl.multiple_of(block * CHUNK, CHUNK), CHUNK)
         return pltpu.make_async_copy(
             forcing.at[:, span, :], forcing_v.at[:, span, :], load_sem.at[block]
         )
 
-    @pl.loop(0, blocks)
+    @pl.loop(0, rows // CHUNK)
     def _(block):
         load(block).start()
 
@@ -99,54 +104,85 @@
     @pl.loop(1, columns)
     def _(shift):
         for rank, value in gather_in(column_at(shift)):
-            send_in[PAIR * shift + rank] = value
+            send_in_a[PAIR * shift + rank] = value[:IN_ROWS]
+            send_in_b[PAIR * shift + rank] = value[IN_ROWS:]
 
     for rank, value in gather_in(me):
-        recv_in[PAIR * me + rank] = value
+        recv_in_a[PAIR * me + rank] = value[:IN_ROWS]
+        recv_in_b[PAIR * me + rank] = value[IN_ROWS:]
+
+    thick_copy.wait()
+    bottom_copy.wait()
+    table_lane = lax.broadcasted_iota(jnp.int32, (TILE, width), 1)
+    depths = jnp.zeros((TILE, width), jnp.float32)
+    for k in range(levels):
+        depths = depths + jnp.where(table_lane > k, thick[k], 0.0)
+    chunk_row = lax.broadcasted_iota(jnp.int32, (CHUNK, width), 0)
+
+    def integrate(chunk):
+        load(chunk).wait()
+        start = pl.multiple_of(chunk * CHUNK, CHUNK)
+        span = pl.ds(start, CHUNK)
+        bottom = bottom_v[span, :]
+        deepest = bottom.astype(jnp.float32).astype(jnp.bfloat16)
+
+        def level(number, source_sum):
+            for step in range(levels // 2):
+                k = number * (levels // 2) + step
+                mark = k.astype(jnp.float32).astype(jnp.bfloat16)
+                layer = jnp.where(deepest > mark, forcing_v[k, span, :], jnp.bfloat16(0))
+                source_sum = source_sum + thick[k] * layer.astype(jnp.float32)
+            return source_sum
+
+        zero = jnp.zeros((CHUNK, width), jnp.float32)
+        source_sum = lax.fori_loop(0, 2, level, zero)
+        depth_sum = jnp.concatenate(
+            [
+                jnp.take_along_axis(depths, bottom[at : at + TILE], axis=1)
+                for at in range(0, CHUNK, TILE)
+            ],
+            axis=0,
+        )
+        wet = jnp.float32(0)
+        for part in range(CHUNK // block_rows):
+            block = chunk * (CHUNK // block_rows) + part
+            here = jnp.where(map_v[me, first_row + block] >= 0, 1.0, 0.0)
+            wet = jnp.where(chunk_row >= part * block_rows, here, wet)
+        here = pl.ds(pl.multiple_of(TILE + start, TILE), CHUNK)
+        nat_half[here, :] = depth_sum * (wet * (0.5 / levels)) + (wet - 1.0)
+        nat_source[here, :] = source_sum * (wet * (1.0 / math.sqrt(levels)))
 
     pl.semaphore_wait(barrier, columns - 1 + len(beside))
 
-    def exchange(shift, sent, received, send_sem, recv_sem):
-        peer = column_at(shift)
+    parts = (
+        (send_in_a, recv_in_a), (send_in_b, recv_in_b),
+        (send_out_a, recv_out_a), (send_out_b, recv_out_b),
+    )
+
+    def exchange(part, shift):
+        sent, received = parts[part]
         return pltpu.make_async_remote_copy(
             src_ref=sent.at[pl.ds(PAIR * shift, PAIR)],
             dst_ref=received.at[pl.ds(PAIR * me, PAIR)],
-            send_sem=send_sem.at[shift],
-            recv_sem=recv_sem.at[shift],
-            device_id=(band, peer),
+            send_sem=exchange_send.at[part, shift],
+            recv_sem=exchange_recv.at[part, shift],
+            device_id=(band, column_at(shift)),
             device_id_type=MESH,
         )
 
-    @pl.loop(1, columns)
-    def _(shift):
-        exchange(shift, send_in, recv_in, in_send, in_recv).start()
-
-    thick_copy.wait()
-    bottom_copy.wait()
-
-    @pl.loop(0, blocks)
-    def _(block):
-        load(block).wait()
-        start = pl.multiple_of(block * block_rows, block_rows)
-        span = pl.ds(start, block_rows)
-        bottom = bottom_v[span, :]
-
-        def level(number, carry):
-            depth_sum, source_sum = carry
-            for step in range(2):
-                k = number * 2 + step
-                layer = forcing_v[k, span, :].astype(jnp.float32)
-                weight = jnp.where(bottom > k, thick[k], 0.0)
-                depth_sum = depth_sum + weight
-                source_sum = source_sum + weight * layer
-            return depth_sum, source_sum
-
-        zero = jnp.zeros((block_rows, width), jnp.float32)
-        depth_sum, source_sum = lax.fori_loop(0, levels // 2, level, (zero, zero))
-        wet = jnp.where(map_v[me, first_row + block] >= 0, 1.0, 0.0)
-        here = pl.ds(pl.multiple_of(TILE + start, TILE), block_rows)
-        nat_half[here, :] = depth_sum * (wet * (0.5 / levels)) + (wet - 1.0)
-        nat_source[here, :] = source_sum * (wet * (1.0 / math.sqrt(levels)))
+    def start_all(part):
+        @pl.loop(1, columns)
+        def _(shift):
+            exchange(part, shift).start()
+
+    def wait_all(part):
+        @pl.loop(1, columns)
+        def _(shift):
+            exchange(part, shift).wait()
+
+    start_all(0)
+    start_all(1)
+    pl.loop(0, rows // CHUNK)(integrate)
 
     def remote(number, src, dst, device):
         return pltpu.make_async_remote_copy(
@@ -158,10 +194,10 @@
             device_id_type=MESH,
         )
 
-    def row_copies(stage, top, bottom, row):
+    def row_copies(number, top, bottom, row):
         return [
             remote(
-                8 * stage + 2 + place,
+                number + place,
                 top if up < 0 else bottom,
                 row.at[place],
                 (band_at(up), column_at(across)),
@@ -169,10 +205,10 @@
             for place, (up, across) in enumerate(beside)
         ]
 
-    def col_copies(stage, strip, col):
+    def col_copies(number, to_left, to_right, col):
         return [
-            remote(8 * stage + side, strip, col.at[side], (band, column_at(across)))
-            for side, across in ((0, -1), (1, 1))
+            remote(number + side, strip, col.at[side], (band, column_at(across)))
+            for side, (strip, across) in enumerate(((to_left, -1), (to_right, 1)))
         ]
 
     has_above = jnp.where(band > 0, 1.0, 0.0)
@@ -192,10 +228,13 @@
         for f in fine:
             field[f, pl.ds(0, width), :] = nat[pl.ds(f, width, stride=FINE), :].T
 
+    def ends_of(field):
+        return field[:, pl.ds(0, TILE), :], field[:, pl.ds(last, TILE), :]
+
     def strip_of(field):
-        return jnp.where(low_rows, field[:, pl.ds(0, TILE), :], field[:, pl.ds(last, TILE), :])
-
-    def fill(nat, field, arrived_row, arrived_col, outside):
+        return jnp.where(low_rows, *ends_of(field))
+
+    def fill(nat, field, arrived_row, halo_columns, outside):
         for at, place, inside in ((above_at, 3, has_above), (below_at, 0, has_below)):
             right, middle, left = (arrived_row(place + k) for k in range(3))
             absent = (1.0 - inside) * outside
@@ -205,7 +244,7 @@
         turn(nat, field, fine_near)
         turned = corner[...].T
         sides = jnp.where(low_row, turned[0:TILE, :], turned[last:width, :])
-        field[:, side_rows, :] = jnp.where(low_rows, arrived_col(0), arrived_col(1))
+        field[:, side_rows, :] = halo_columns
         for n, lane in near:
             f, to = n % FINE, n // FINE
             moved = pltpu.roll(sides, (to - lane) % width, 1)
@@ -220,9 +259,10 @@
         copy.start()
     turn(nat_half, raw, range(FINE))
     turn(nat_source, source, range(FINE))
-    strip_first[0] = strip_of(raw)
-    strip_first[1] = strip_of(source)
-    first_cols = col_copies(0, strip_first, col_first)
+    (raw_start, raw_end), (source_start, source_end) = ends_of(raw), ends_of(source)
+    strip_first[0] = jnp.where(low_rows, raw_start, pltpu.roll(source_start, HALO, 1))
+    strip_first[1] = jnp.where(low_rows, pltpu.roll(source_end, HALO, 1), raw_end)
+    first_cols = col_copies(6, strip_first.at[0], strip_first.at[1], col_first)
     for copy in first_cols:
         copy.start()
 
@@ -255,8 +295,10 @@
 
     for copy in first_rows + first_cols:
         copy.wait()
-    fill(nat_half, raw, lambda p: row_first[p, 0], lambda s: col_first[s, 0], -1.0)
-    fill(nat_source, source, lambda p: row_first[p, 1], lambda s: col_first[s, 1], 0.0)
+    raw_halo = jnp.where(low_rows, col_first[0], col_first[1])
+    source_halo = pltpu.roll(jnp.where(low_rows, col_first[1], col_first[0]), HALO, 1)
+    fill(nat_half, raw, lambda p: row_first[p, 0], raw_halo, -1.0)
+    fill(nat_source, source, lambda p: row_first[p, 1], source_halo, 0.0)
 
     tiles = width // TILE + 1
 
@@ -290,69 +332,104 @@
         wet = raw[:, tile_at(tile), :] >= 0.0
         inverse[:, tile_at(tile), :] = jnp.where(wet, 1.0 / diagonal, 0.0)
 
-    @pl.loop(1, columns)
-    def _(shift):
-        exchange(shift, send_in, recv_in, in_send, in_recv).wait()
-
-    for block in range(blocks):
-        wet = jnp.where(map_v[me, first_row + block] >= 0, 1.0, 0.0)
-        nat_eta[pl.ds(TILE + block * block_rows, block_rows), :] = recv_in[t_clinic[block]] * wet
-
-    second_rows = row_copies(
-        1, nat_eta.at[pl.ds(TILE, TILE)], nat_eta.at[pl.ds(rows, TILE)], row_eta
-    )
-    for copy in second_rows:
-        copy.start()
-    turn(nat_eta, eta, range(FINE))
-    strip_eta[...] = strip_of(eta)
-    second_cols = col_copies(1, strip_eta, col_eta)
-    for copy in second_cols:
-        copy.start()
-    for copy in second_rows + second_cols:
-        copy.wait()
-    fill(nat_eta, eta, lambda p: row_eta[p], lambda s: col_eta[s], 0.0)
-    for tile in range(tiles):
-        here = tile_at(tile)
-        rhs[:, here, :] = (SURFACE + 2.0 * half[:, here, :]) * eta[:, here, :] + source[:, here, :]
-
-    @pl.loop(0, ITERS)
-    def _(iteration):
+    def sweeps(eta):
         for tile in range(tiles):
             here = tile_at(tile)
-            value, weight = eta[:, here, :], half[:, here, :]
-            scaled = value * weight
-            around, scaled_around = row_sum(value), row_sum(scaled)
-            put(g_eta, tile, value + 0.5 * around)
-            put(g_half, tile, scaled + 0.5 * scaled_around)
-            rest[:, here, :] = rhs[:, here, :] + weight * around + scaled_around
-        for tile in range(tiles):
-            here = tile_at(tile)
-            total = rest[:, here, :] + col_sum(g_half, tile)
-            total = total + half[:, here, :] * col_sum(g_eta, tile)
-            eta[:, here, :] = total * inverse[:, here, :]
-
-    for f in range(FINE):
-        nat_half[pl.ds(f, width, stride=FINE), :] = eta[f, pl.ds(0, width), :].T
+            rhs[:, here, :] = (SURFACE + 2.0 * half[:, here, :]) * eta[:, here, :] + source[
+                :, here, :
+            ]
+
+        @pl.loop(0, ITERS)
+        def _(iteration):
+            for tile in range(tiles):
+                here = tile_at(tile)
+                value, weight = eta[:, here, :], half[:, here, :]
+                scaled = value * weight
+                around, scaled_around = row_sum(value), row_sum(scaled)
+                put(g_eta, tile, value + 0.5 * around)
+                put(g_half, tile, scaled + 0.5 * scaled_around)
+                rest[:, here, :] = rhs[:, here, :] + weight * around + scaled_around
+            for tile in range(tiles):
+                here = tile_at(tile)
+                total = rest[:, here, :] + col_sum(g_half, tile)
+                total = total + half[:, here, :] * col_sum(g_eta, tile)
+                eta[:, here, :] = total * inverse[:, here, :]
+
+        for f in range(FINE):
+            nat_half[pl.ds(f, width, stride=FINE), :] = eta[f, pl.ds(0, width), :].T
+
+    def unpack(part, received, at, count):
+        wait_all(part)
+        for block in range(blocks):
+            wet = jnp.where(map_v[me, first_row + block] >= 0, 1.0, 0.0)
+            there = pl.ds(TILE + block * block_rows + at, count)
+            nat_eta[there, :] = received[t_clinic[block]] * wet
+
+    def send_back(part, end):
+        sent, received = parts[part]
+
+        @pl.loop(1, columns)
+        def _(shift):
+            peer = column_at(shift)
+            for rank in range(PAIR):
+                sent[PAIR * shift + rank] = end[t_out[PAIR * peer + rank]]
+            exchange(part, shift).start()
+
+        for rank in range(PAIR):
+            received[PAIR * me + rank] = end[t_out[PAIR * me + rank]]
+
+    unpack(0, recv_in_a, 0, IN_ROWS)
+    turn(nat_eta, eta_a, range(FINE))
+    strip_eta[0] = strip_of(eta_a)
+    cols_a = col_copies(8, strip_eta.at[0], strip_eta.at[0], col_eta.at[0])
+    for copy in cols_a:
+        copy.start()
+
+    unpack(1, recv_in_b, IN_ROWS, block_rows - IN_ROWS)
+    rows_b = row_copies(10, nat_eta.at[pl.ds(TILE, TILE)], nat_eta.at[pl.ds(rows, TILE)], row_eta)
+    for copy in rows_b:
+        copy.start()
+    turn(nat_eta, eta_b, range(FINE))
+    strip_eta[1] = strip_of(eta_b)
+    cols_b = col_copies(16, strip_eta.at[1], strip_eta.at[1], col_eta.at[1])
+    for copy in cols_b:
+        copy.start()
+
+    for copy in cols_a:
+        copy.wait()
+    eta_a[:, side_rows, :] = jnp.where(low_rows, col_eta[0, 0], col_eta[0, 1])
+    sweeps(eta_a)
     for block in range(blocks):
-        eta_end[block] = nat_half[pl.ds(TILE + block * block_rows, block_rows), :]
-
-    @pl.loop(1, columns)
-    def _(shift):
-        peer = column_at(shift)
-        for rank in range(PAIR):
-            send_out[PAIR * shift + rank] = eta_end[t_out[PAIR * peer + rank]]
-        exchange(shift, send_out, recv_out, out_send, out_recv).start()
-
-    for rank in range(PAIR):
-        recv_out[PAIR * me + rank] = eta_end[t_out[PAIR * me + rank]]
-
-    @pl.loop(1, columns)
-    def _(shift):
-        exchange(shift, send_out, recv_out, out_send, out_recv).wait()
+        end_a[block] = nat_half[pl.ds(TILE + block * block_rows + OUT_ROW, OUT_ROWS), :]
+    send_back(2, end_a)
+
+    for copy in rows_b + cols_b:
+        copy.wait()
+    halo_b = jnp.where(low_rows, col_eta[1, 0], col_eta[1, 1])
+    fill(nat_eta, eta_b, lambda p: row_eta[p], halo_b, 0.0)
+    sweeps(eta_b)
+    behind = block_rows - OUT_ROW - OUT_ROWS
+    for block in range(blocks):
+        start = TILE + block * block_rows
+        end_b[block, pl.ds(0, behind), :] = nat_half[
+            pl.ds(start + OUT_ROW + OUT_ROWS, behind), :
+        ]
+        end_b[block, pl.ds(behind, OUT_ROW), :] = nat_half[pl.ds(start, OUT_ROW), :]
+    send_back(3, end_b)
+
+    wait_all(2)
 
     @pl.loop(0, slots)
     def _(slot):
-        eta_next[0, slot] = recv_out[t_owner[slot]]
+        eta_next[0, slot, pl.ds(OUT_ROW, OUT_ROWS), :] = recv_out_a[t_owner[slot]]
+
+    wait_all(3)
+
+    @pl.loop(0, slots)
+    def _(slot):
+        value = recv_out_b[t_owner[slot]]
+        eta_next[0, slot, pl.ds(OUT_ROW + OUT_ROWS, behind), :] = value[:behind]
+        eta_next[0, slot, pl.ds(0, OUT_ROW), :] = value[behind:]
 
 
 def solution(mesh):
@@ -377,22 +454,22 @@
             pltpu.VMEM((rows, width), jnp.int32),
             vmem(slots, block_rows, width),
         ]
-        scratch += [vmem(PAIR * columns, block_rows, width)] * 4
-        scratch += [vmem(blocks, block_rows, width)]
+        for count in (IN_ROWS, block_rows - IN_ROWS, OUT_ROWS, block_rows - OUT_ROWS):
+            scratch += [vmem(PAIR * columns, count, width)] * 2
+        scratch += [vmem(blocks, OUT_ROWS, width), vmem(blocks, block_rows - OUT_ROWS, width)]
         scratch += [vmem(FINE * width, width)] * 3 + [vmem(width, width)]
-        scratch += [vmem(FINE, tall, width)] * 7
+        scratch += [vmem(FINE, tall, width)] * 8
         scratch += [vmem(FINE, tall + 2 * TILE, width)] * 2
-        scratch += [vmem(2, FINE, TILE, width), vmem(FINE, TILE, width)]
-        scratch += [vmem(2, 2, FINE, TILE, width), vmem(2, FINE, TILE, width)]
+        scratch += [vmem(2, FINE, TILE, width)] * 3 + [vmem(2, 2, FINE, TILE, width)]
         scratch += [vmem(2, 2, TILE, width), vmem(6, 2, TILE, width), vmem(6, TILE, width)]
         scratch += [smem(*tropic_map.shape[::-1]), pltpu.SMEM((levels,), f32)]
         scratch += [
             smem(PAIR * columns), smem(blocks), smem(PAIR * columns), smem(slots), smem(blocks)
         ]
-        scratch += [dma((blocks,))] + [dma] * 4 + [dma((columns,))] * 4 + [dma((16,))] * 2
+        scratch += [dma((rows // CHUNK,))] + [dma] * 4 + [dma((4, columns))] * 2 + [dma((18,))] * 2
         return pl.pallas_call(
             functools.partial(kernel, sizes),
-            out_shape=jax.ShapeDtypeStruct(eta_prev.shape, f32),
+            out_shape=pltpu.VMEM(eta_prev.shape, f32),
             in_specs=[pl.BlockSpec(memory_space=pl.ANY)] * 5,
             out_specs=pl.BlockSpec(memory_space=pltpu.VMEM),
             scratch_shapes=scratch,

time: 50.5 us -> 44.5 us (0.88); the launches traced: 50.4 us -> 43.9 us
  Pallas kernels: 48.6 us -> 43.1 us
  local copies, waits for them, and re-layouts: 1.82 us -> 0.77 us
    pallas_call x1, Pallas kernels: 48.6 us -> 43.1 us  [body(): pl.pallas_call(functools.partial(kernel, sizes), out_shape=pltpu.VMEM(eta...]
    unnamed x1, local copies, waits for them, and re-layouts: 1.82 us -> 0.77 us
where the time goes in v3:
time: 44.5 us; the launch traced here: 43.9 us
  Pallas kernels  43.1 us (97%)
  local copies, waits for them, and re-layouts  0.77 us (2%)
    pallas_call x1, Pallas kernels, body(): pl.pallas_call(functools.partial(kernel, sizes), out_shape=pltpu.VMEM(eta...  43.1 us

profile of v3, /device:TPU:1, one launch (start us, length us, event | category | flops | bytes accessed | tf_op | source)
XLA Modules:
  0.0 43.9 jit_solution(8960869235194923103)
XLA Ops:
  0.0 43.1 %shard_map.55 = f32[1,14,64,128]{3,2,1,0:T(8,128)S(1)} custom-call(s32[16,128]{1,0:T(8,128)} %bitcast.1, f32[62]{0:T(128)} %thickness.1, bf16[62,1024,128]{2,1,0:T(8,128)(2,1)} %forcing.1, s32[1024,128]{1,0:T(8,128)} %bottom_level.1, f32[1,14,64,128]{3,2,1,0:T(8,128)} %eta_prev.1), custom_call_target="tpu_custom_call" | custom-call | flops 60000000 | bytes 18000000 | tf_op jit(solution)/shard_map/pallas_call | solution.py:470
  43.1 0.8 %copy.7 = f32[1,14,64,128]{3,2,1,0:T(8,128)} copy(f32[1,14,64,128]{3,2,1,0:T(8,128)S(1)} %shard_map.55) | data formatting | bytes 917504

commit v4 on v3

--- a/solution.py
+++ b/solution.py
@@ -293,13 +293,6 @@
             place = jnp.where(t_in[entry] == slot, entry, place)
         t_owner[slot] = place
 
-    for copy in first_rows + first_cols:
-        copy.wait()
-    raw_halo = jnp.where(low_rows, col_first[0], col_first[1])
-    source_halo = pltpu.roll(jnp.where(low_rows, col_first[1], col_first[0]), HALO, 1)
-    fill(nat_half, raw, lambda p: row_first[p, 0], raw_halo, -1.0)
-    fill(nat_source, source, lambda p: row_first[p, 1], source_halo, 0.0)
-
     tiles = width // TILE + 1
 
     def tile_at(tile):
@@ -320,17 +313,6 @@
     def col_sum(field, tile):
         start = TILE * (tile + 1)
         return field[:, pl.ds(start - 1, TILE), :] + field[:, pl.ds(start + 1, TILE), :]
-
-    for tile in range(tiles):
-        value = jnp.maximum(raw[:, tile_at(tile), :], 0.0)
-        half[:, tile_at(tile), :] = value
-        around = row_sum(value)
-        put(g_half, tile, value + 0.5 * around)
-        rest[:, tile_at(tile), :] = (SURFACE + 8.0 * value) + around
-    for tile in range(tiles):
-        diagonal = rest[:, tile_at(tile), :] + col_sum(g_half, tile)
-        wet = raw[:, tile_at(tile), :] >= 0.0
-        inverse[:, tile_at(tile), :] = jnp.where(wet, 1.0 / diagonal, 0.0)
 
     def sweeps(eta):
         for tile in range(tiles):
@@ -385,6 +367,7 @@
     for copy in cols_a:
         copy.start()
 
+
     unpack(1, recv_in_b, IN_ROWS, block_rows - IN_ROWS)
     rows_b = row_copies(10, nat_eta.at[pl.ds(TILE, TILE)], nat_eta.at[pl.ds(rows, TILE)], row_eta)
     for copy in rows_b:
@@ -394,6 +377,23 @@
     cols_b = col_copies(16, strip_eta.at[1], strip_eta.at[1], col_eta.at[1])
     for copy in cols_b:
         copy.start()
+
+    for copy in first_rows + first_cols:
+        copy.wait()
+    raw_halo = jnp.where(low_rows, col_first[0], col_first[1])
+    source_halo = pltpu.roll(jnp.where(low_rows, col_first[1], col_first[0]), HALO, 1)
+    fill(nat_half, raw, lambda p: row_first[p, 0], raw_halo, -1.0)
+    fill(nat_source, source, lambda p: row_first[p, 1], source_halo, 0.0)
+    for tile in range(tiles):
+        value = jnp.maximum(raw[:, tile_at(tile), :], 0.0)
+        half[:, tile_at(tile), :] = value
+        around = row_sum(value)
+        put(g_half, tile, value + 0.5 * around)
+        rest[:, tile_at(tile), :] = (SURFACE + 8.0 * value) + around
+    for tile in range(tiles):
+        diagonal = rest[:, tile_at(tile), :] + col_sum(g_half, tile)
+        wet = raw[:, tile_at(tile), :] >= 0.0
+        inverse[:, tile_at(tile), :] = jnp.where(wet, 1.0 / diagonal, 0.0)
 
     for copy in cols_a:
         copy.wait()

time: 44.5 us -> 42.4 us (0.953); the launches traced: 43.9 us -> 42.3 us
  Pallas kernels: 43.1 us -> 41.5 us
    pallas_call x1, Pallas kernels: 43.1 us -> 41.5 us  [body(): pl.pallas_call(functools.partial(kernel, sizes), out_shape=pltpu.VMEM(eta...]
where the time goes in v4:
time: 42.4 us; the launch traced here: 42.3 us
  Pallas kernels  41.5 us (98%)
  local copies, waits for them, and re-layouts  0.77 us (2%)
    pallas_call x1, Pallas kernels, body(): pl.pallas_call(functools.partial(kernel, sizes), out_shape=pltpu.VMEM(eta...  41.5 us

profile of v4, /device:TPU:1, one launch (start us, length us, event | category | flops | bytes accessed | tf_op | source)
XLA Modules:
  0.0 42.3 jit_solution(5227046860005482820)
XLA Ops:
  0.0 41.5 %shard_map.55 = f32[1,14,64,128]{3,2,1,0:T(8,128)S(1)} custom-call(s32[16,128]{1,0:T(8,128)} %bitcast.1, f32[62]{0:T(128)} %thickness.1, bf16[62,1024,128]{2,1,0:T(8,128)(2,1)} %forcing.1, s32[1024,128]{1,0:T(8,128)} %bottom_level.1, f32[1,14,64,128]{3,2,1,0:T(8,128)} %eta_prev.1), custom_call_target="tpu_custom_call" | custom-call | flops 60000000 | bytes 18000000 | tf_op jit(solution)/shard_map/pallas_call | solution.py:470
  41.5 0.8 %copy.7 = f32[1,14,64,128]{3,2,1,0:T(8,128)} copy(f32[1,14,64,128]{3,2,1,0:T(8,128)S(1)} %shard_map.55) | data formatting | bytes 917504

commit v5 on v4

--- a/solution.py
+++ b/solution.py
@@ -77,9 +77,13 @@
             forcing.at[:, span, :], forcing_v.at[:, span, :], load_sem.at[block]
         )
 
-    @pl.loop(0, rows // CHUNK)
-    def _(block):
-        load(block).start()
+    chunks = rows // CHUNK
+    load(0).start()
+    load(chunks - 1).start()
+
+    @pl.loop(1, chunks - 1)
+    def _(chunk):
+        load(chunk).start()
 
     map_copy.wait()
 
@@ -182,8 +186,6 @@
 
     start_all(0)
     start_all(1)
-    pl.loop(0, rows // CHUNK)(integrate)
-
     def remote(number, src, dst, device):
         return pltpu.make_async_remote_copy(
             src_ref=src,
@@ -250,6 +252,7 @@
             moved = pltpu.roll(sides, (to - lane) % width, 1)
             field[f, side_rows, :] = jnp.where(tile_lane == to, moved, field[f, side_rows, :])
 
+    pl.loop(0, 2)(lambda end: integrate(end * (chunks - 1)))
     corner[...] = jnp.zeros_like(corner)
     for number, nat in enumerate((nat_half, nat_source)):
         edge_first[0, number] = nat[pl.ds(TILE, TILE), :]
@@ -257,6 +260,7 @@
     first_rows = row_copies(0, edge_first.at[0], edge_first.at[1], row_first)
     for copy in first_rows:
         copy.start()
+    pl.loop(1, chunks - 1)(integrate)
     turn(nat_half, raw, range(FINE))
     turn(nat_source, source, range(FINE))
     (raw_start, raw_end), (source_start, source_end) = ends_of(raw), ends_of(source)

time: 42.4 us -> 42.1 us (level)
  no operation moved by 1% of the time
where the time goes in v5:
time: 42.1 us; the launch traced here: 42 us
  Pallas kernels  41.2 us (98%)
  local copies, waits for them, and re-layouts  0.77 us (2%)
    pallas_call x1, Pallas kernels, body(): pl.pallas_call(functools.partial(kernel, sizes), out_shape=pltpu.VMEM(eta...  41.2 us

profile of v5, /device:TPU:1, one launch (start us, length us, event | category | flops | bytes accessed | tf_op | source)
XLA Modules:
  0.0 42.0 jit_solution(17408286483815694585)
XLA Ops:
  0.0 41.2 %shard_map.55 = f32[1,14,64,128]{3,2,1,0:T(8,128)S(1)} custom-call(s32[16,128]{1,0:T(8,128)} %bitcast.1, f32[62]{0:T(128)} %thickness.1, bf16[62,1024,128]{2,1,0:T(8,128)(2,1)} %forcing.1, s32[1024,128]{1,0:T(8,128)} %bottom_level.1, f32[1,14,64,128]{3,2,1,0:T(8,128)} %eta_prev.1), custom_call_target="tpu_custom_call" | custom-call | flops 60000000 | bytes 18000000 | tf_op jit(solution)/shard_map/pallas_call | solution.py:474
  41.3 0.8 %copy.7 = f32[1,14,64,128]{3,2,1,0:T(8,128)} copy(f32[1,14,64,128]{3,2,1,0:T(8,128)S(1)} %shard_map.55) | data formatting | bytes 917504

commit v6 on v5

--- a/solution.py
+++ b/solution.py
@@ -233,8 +233,29 @@
     def ends_of(field):
         return field[:, pl.ds(0, TILE), :], field[:, pl.ds(last, TILE), :]
 
-    def strip_of(field):
-        return jnp.where(low_rows, *ends_of(field))
+    many = (FINE + 1) // 2
+
+    def paired(end):
+        return jnp.concatenate([pltpu.roll(end[many:], HALO, 1), end[many - 1 : many]], axis=0)
+
+    def strips_of(field):
+        start, end = ends_of(field)
+        low = low_rows[:many]
+        return (
+            jnp.where(low, start[:many], paired(start)),
+            jnp.where(low, paired(end), end[:many]),
+        )
+
+    def halo_of(right, left):
+        rest_right = pltpu.roll(right[: FINE - many], HALO, 1)
+        rest_left = pltpu.roll(left[: FINE - many], HALO, 1)
+        return jnp.concatenate(
+            [
+                jnp.where(low_rows[:many], right, left),
+                jnp.where(low_rows[many:], rest_right, rest_left),
+            ],
+            axis=0,
+        )
 
     def fill(nat, field, arrived_row, halo_columns, outside):
         for at, place, inside in ((above_at, 3, has_above), (below_at, 0, has_below)):
@@ -366,8 +387,8 @@
 
     unpack(0, recv_in_a, 0, IN_ROWS)
     turn(nat_eta, eta_a, range(FINE))
-    strip_eta[0] = strip_of(eta_a)
-    cols_a = col_copies(8, strip_eta.at[0], strip_eta.at[0], col_eta.at[0])
+    strip_eta[0, 0], strip_eta[0, 1] = strips_of(eta_a)
+    cols_a = col_copies(8, strip_eta.at[0, 0], strip_eta.at[0, 1], col_eta.at[0])
     for copy in cols_a:
         copy.start()
 
@@ -377,8 +398,8 @@
     for copy in rows_b:
         copy.start()
     turn(nat_eta, eta_b, range(FINE))
-    strip_eta[1] = strip_of(eta_b)
-    cols_b = col_copies(16, strip_eta.at[1], strip_eta.at[1], col_eta.at[1])
+    strip_eta[1, 0], strip_eta[1, 1] = strips_of(eta_b)
+    cols_b = col_copies(16, strip_eta.at[1, 0], strip_eta.at[1, 1], col_eta.at[1])
     for copy in cols_b:
         copy.start()
 
@@ -401,7 +422,7 @@
 
     for copy in cols_a:
         copy.wait()
-    eta_a[:, side_rows, :] = jnp.where(low_rows, col_eta[0, 0], col_eta[0, 1])
+    eta_a[:, side_rows, :] = halo_of(col_eta[0, 0], col_eta[0, 1])
     sweeps(eta_a)
     for block in range(blocks):
         end_a[block] = nat_half[pl.ds(TILE + block * block_rows + OUT_ROW, OUT_ROWS), :]
@@ -409,7 +430,7 @@
 
     for copy in rows_b + cols_b:
         copy.wait()
-    halo_b = jnp.where(low_rows, col_eta[1, 0], col_eta[1, 1])
+    halo_b = halo_of(col_eta[1, 0], col_eta[1, 1])
     fill(nat_eta, eta_b, lambda p: row_eta[p], halo_b, 0.0)
     sweeps(eta_b)
     behind = block_rows - OUT_ROW - OUT_ROWS
@@ -429,8 +450,7 @@
 
     wait_all(3)
 
-    @pl.loop(0, slots)
-    def _(slot):
+    for slot in range(slots):
         value = recv_out_b[t_owner[slot]]
         eta_next[0, slot, pl.ds(OUT_ROW + OUT_ROWS, behind), :] = value[:behind]
         eta_next[0, slot, pl.ds(0, OUT_ROW), :] = value[behind:]
@@ -464,7 +484,7 @@
         scratch += [vmem(FINE * width, width)] * 3 + [vmem(width, width)]
         scratch += [vmem(FINE, tall, width)] * 8
         scratch += [vmem(FINE, tall + 2 * TILE, width)] * 2
-        scratch += [vmem(2, FINE, TILE, width)] * 3 + [vmem(2, 2, FINE, TILE, width)]
+        scratch += [vmem(2, FINE, TILE, width)] * 2 + [vmem(2, 2, (FINE + 1) // 2, TILE, width)] * 2
         scratch += [vmem(2, 2, TILE, width), vmem(6, 2, TILE, width), vmem(6, TILE, width)]
         scratch += [smem(*tropic_map.shape[::-1]), pltpu.SMEM((levels,), f32)]
         scratch += [

time: 42.1 us -> 41.9 us (level)
  no operation moved by 1% of the time
where the time goes in v6:
time: 41.9 us; the launch traced here: 41.8 us
  Pallas kernels  41 us (98%)
  local copies, waits for them, and re-layouts  0.77 us (2%)
    pallas_call x1, Pallas kernels, body(): pl.pallas_call(functools.partial(kernel, sizes), out_shape=pltpu.VMEM(eta...  41 us

profile of v6, /device:TPU:1, one launch (start us, length us, event | category | flops | bytes accessed | tf_op | source)
XLA Modules:
  0.0 41.8 jit_solution(3766610310141680519)
XLA Ops:
  0.0 41.0 %shard_map.55 = f32[1,14,64,128]{3,2,1,0:T(8,128)S(1)} custom-call(s32[16,128]{1,0:T(8,128)} %bitcast.1, f32[62]{0:T(128)} %thickness.1, bf16[62,1024,128]{2,1,0:T(8,128)(2,1)} %forcing.1, s32[1024,128]{1,0:T(8,128)} %bottom_level.1, f32[1,14,64,128]{3,2,1,0:T(8,128)} %eta_prev.1), custom_call_target="tpu_custom_call" | custom-call | flops 60000000 | bytes 18000000 | tf_op jit(solution)/shard_map/pallas_call | solution.py:494
  41.0 0.8 %copy.7 = f32[1,14,64,128]{3,2,1,0:T(8,128)} copy(f32[1,14,64,128]{3,2,1,0:T(8,128)S(1)} %shard_map.55) | data formatting | bytes 917504
